TPU v7x, 32 devices: a whole 2x2x4 slice. The times are simulated.
32 devices in a mesh: prow: 4 (over y, core), pcol: 8 (over z, x).
Axes of the slice: x: 2, y: 2, z: 4, core: 2. Of those that a mesh axis runs over, the one named last changes fastest.
Arguments:
- ainv: bfloat16 [4096, 4096], P('pcol', 'prow'), may hold values from -6 to 6
- lpanel: bfloat16 [4096, 2048], P('prow', 'pcol'), may hold values from -0.125 to 0.125
- dinv: float32 [256, 2048], P(None, 'prow'), may hold values from -6 to 6
- rowblocks: int32 [8, 10], replicated, may hold values from 0 to 15, as said below
- counts: int32 [8], replicated, may hold values from 7 to 10
- widths: int32 [8], replicated, may hold values from 1 to 256, 1536 in all
Outputs:
- selected_inverse: bfloat16 [4096, 2048], P('pcol', 'prow')
- diagonal_blocks: float32 [256, 2048], P(None, 'prow')
Inputs may be any that keep to these rules, and one draw needn't show every extreme that they name: The entries of one row of rowblocks are distinct; only the first counts[k] entries of row k belong to supernode k. The widths sum to 1536.
All inputs are finite; a program needn't handle non-finite values.
Results may differ from a plain program's by a relative error of at most 0.02.
Values may be sent and summed in bfloat16 or wider, within the bound.
A program may use at most 64 MiB of HBM per device.

v0:
```python
import jax
import jax.numpy as jnp
from jax import lax
from jax.sharding import PartitionSpec as P

B = 256
SNODES = 8


def from_root(value, axis, source):
    kept = jnp.where(lax.axis_index(axis) == source, value, 0).astype(value.dtype)
    return lax.psum(kept, axis)


def block_mask(block_ids, column_ids, rowblocks, counts, widths):
    slot_total = rowblocks.shape[1]
    owner_node = column_ids // B
    within = column_ids % B
    chosen = owner_node[:, None] == jnp.arange(SNODES, dtype=jnp.int32)[None, :]
    owner_rows = jnp.sum(jnp.where(chosen[:, :, None], rowblocks[None, :, :], 0), axis=1)
    owner_count = jnp.sum(jnp.where(chosen, counts[None, :], 0), axis=1)
    owner_width = jnp.sum(jnp.where(chosen, widths[None, :], 0), axis=1)
    slot_live = jnp.arange(slot_total, dtype=jnp.int32)[None, :] < owner_count[:, None]
    matched = (owner_rows[None, :, :] == block_ids[:, None, None]) & slot_live[None, :, :]
    present = jnp.any(matched, axis=2) & (within < owner_width)[None, :]
    return (present, owner_width, within)


def per_device(ainv, lpanel, dinv, rowblocks, counts, widths):
    row_group = lax.axis_index("prow")
    col_group = lax.axis_index("pcol")
    panel_rows = lpanel.shape[0]
    panel_cols = lpanel.shape[1]
    inverse_rows = ainv.shape[0]
    share_cols = dinv.shape[1]
    row_blocks = panel_rows // B
    col_blocks = inverse_rows // B
    own_ids = row_group * row_blocks + jnp.arange(row_blocks, dtype=jnp.int32)
    own_cols = col_group * panel_cols + jnp.arange(panel_cols, dtype=jnp.int32)
    present, unused_width, unused_within = block_mask(own_ids, own_cols, rowblocks, counts, widths)
    masked = jnp.where(
        present[:, None, :], lpanel.reshape(row_blocks, B, panel_cols), jnp.zeros((), jnp.bfloat16)
    )
    masked = masked.reshape(panel_rows, panel_cols)
    gathered = lax.all_gather(masked, "pcol", axis=1, tiled=True)
    product = jnp.dot(ainv, gathered, preferred_element_type=jnp.float32)
    root_row = col_group * col_blocks // row_blocks
    offset = (col_group * col_blocks - root_row * row_blocks) * B
    own_rows = lax.dynamic_slice_in_dim(gathered, offset, inverse_rows, 0)
    width_cols = max(share_cols, B)
    first_col = row_group * share_cols // width_cols * width_cols
    summed = lax.psum_scatter(
        product.astype(jnp.bfloat16), "prow", scatter_dimension=1, tiled=True
    ).astype(jnp.float32)
    whole_rows = from_root(own_rows, "prow", root_row)
    across = lax.dynamic_slice_in_dim(whole_rows, first_col, width_cols, 1)
    column_ids = row_group * share_cols + jnp.arange(share_cols, dtype=jnp.int32)
    block_ids = col_group * col_blocks + jnp.arange(col_blocks, dtype=jnp.int32)
    kept, owner_width, within = block_mask(block_ids, column_ids, rowblocks, counts, widths)
    negated = jnp.where(
        kept[:, None, :], -summed.reshape(col_blocks, B, share_cols), jnp.zeros((), jnp.float32)
    )
    selected_inverse = negated.reshape(inverse_rows, share_cols).astype(jnp.bfloat16)
    groups = max(1, share_cols // B)
    left_side = across.reshape(inverse_rows, groups, width_cols // groups).astype(jnp.float32)
    right_side = summed.reshape(inverse_rows, groups, share_cols // groups)
    quadratic = jnp.einsum(
        "rnb,rnc->bnc", left_side, right_side, precision=lax.Precision.HIGHEST
    ).reshape(B, share_cols)
    quadratic = lax.psum(quadratic.astype(jnp.bfloat16), "pcol").astype(jnp.float32)
    corner = (jnp.arange(B, dtype=jnp.int32)[:, None] < owner_width[None, :]) & (
        within < owner_width
    )[None, :]
    diagonal_blocks = jnp.where(corner, dinv, jnp.zeros((), jnp.float32)) + quadratic
    return (selected_inverse, diagonal_blocks)


def solution(mesh):
    placed = (P("pcol", "prow"), P("prow", "pcol"), P(None, "prow"), P(), P(), P())
    return jax.shard_map(
        per_device,
        mesh=mesh,
        in_specs=placed,
        out_specs=(P("pcol", "prow"), P(None, "prow")),
        check_vma=False,
    )
```

profile of v0, /device:TPU:0, one launch (start us, length us, event | category | flops | bytes accessed | tf_op | source)
XLA Modules:
  0.0 258.4 jit_solution(10271501812665565915)
XLA Ops:
  7.2 0.8 copy.15
  8.1 0.8 select_reduce_fusion.4
  9.0 0.1 and_reduce_fusion.1
  9.1 0.2 copy.17
  9.3 0.4 broadcast_in_dim.155
  9.8 0.1 copy.24
  9.9 1.2 copy.18
  11.1 0.8 broadcast_select_fusion
  12.1 76.2 %all-gather.2.cloned.1.call-done = bf16[1024,2048]{0,1:T(8,128)(2,1)} async-done(((bf16[1024,256]{0,1:T(8,128)(2,1)}), bf16[1024,2048]{0,1:T(8,128)(2,1)}) %all-gather.2.cloned.1.call-update) | async-done | bytes 4194320 | tf_op jit(solution)/shard_map/all_gather | solution.py:45
  88.3 3.3 %dynamic-slice_select_fusion = bf16[512,2048]{0,1:T(8,128)(2,1)} fusion(bf16[1024,2048]{0,1:T(8,128)(2,1)} %all-gather.2.cloned.1.call-done, s32[]{:T(128)S(6)} %select_n.111, pred[]{:T(512)S(6)} %eq.79), kind=kLoop, calls=%fused_computation.2 | loop fusion | flops 1048576 | bytes 4194309 | tf_op jit(solution)/shard_map/jit(_where)/select_n | solution.py:11
  91.7 5.9 %fusion = bf16[512,2048]{0,1:T(8,128)(2,1)} fusion(bf16[1024,2048]{0,1:T(8,128)(2,1)} %all-gather.2.cloned.1.call-done, bf16[512,1024]{1,0:T(8,128)(2,1)S(1)} %copy-done), kind=kOutput, calls=%fused_computation.1 | convolution fusion | flops 2148532224 | bytes 7340032 | tf_op jit(solution)/shard_map/dot_general | solution.py:46
  97.7 0.5 copy-done.3
  98.4 0.1 select_reduce_fusion
  98.5 0.1 and_reduce_fusion
  98.6 42.8 %all-reduce.3.cloned.1.call-done = bf16[512,2048]{0,1:T(8,128)(2,1)} async-done(((bf16[512,2048]{0,1:T(8,128)(2,1)}), bf16[512,2048]{0,1:T(8,128)(2,1)}) %all-reduce.3.cloned.1.call-update) | async-done | bytes 2097168 | tf_op jit(solution)/shard_map/psum | solution.py:12
  141.4 1.1 constant_dynamic-slice_fusion
  142.5 33.1 %reduce-scatter.2.cloned.1.call-done = bf16[512,512]{0,1:T(8,128)(2,1)} async-done(((bf16[512,2048]{0,1:T(8,128)(2,1)}), bf16[512,512]{0,1:T(8,128)(2,1)}) %reduce-scatter.2.cloned.1.call-update) | async-done | bytes 524304 | tf_op jit(solution)/shard_map/reduce_scatter | solution.py:52
  175.6 1.4 convolution_convert_fusion.1
  177.1 0.8 copy.21
  178.1 0.4 copy.19
  178.5 0.2 select_convert_fusion
  178.7 1.0 copy.22
  179.7 70.3 %all-reduce.5.cloned.1.call-done = bf16[256,512]{1,0:T(8,128)(2,1)} async-done(((bf16[256,512]{1,0:T(8,128)(2,1)}), bf16[256,512]{1,0:T(8,128)(2,1)}) %all-reduce.5.cloned.1.call-update) | async-done | bytes 262160 | tf_op jit(solution)/shard_map/psum | solution.py:70
  250.0 1.9 convert_add_fusion
  (32 shorter events, 0.6 us)
Async XLA Ops:
  7.2 84.5 %copy-start = (bf16[512,1024]{1,0:T(8,128)(2,1)S(1)}, bf16[512,1024]{1,0:T(8,128)(2,1)}, u32[]{:S(2)}) copy-start(bf16[512,1024]{1,0:T(8,128)(2,1)} %param.6) | copy-start | bytes 3145732
  7.2 81.1 %all-gather.2.cloned.1.call-start = ((), (), s32[]{:S(2)}) async-start(), calls=%async_computation.1 | async-start | bytes 4718592 | tf_op jit(solution)/shard_map/all_gather | solution.py:45
  12.0 129.4 %all-reduce.3.cloned.1.call-start = ((), (), s32[]{:S(2)}) async-start(), calls=%async_computation.3 | async-start | bytes 4194304 | tf_op jit(solution)/shard_map/psum | solution.py:12
  91.6 84.0 %reduce-scatter.2.cloned.1.call-start = ((), (), s32[]{:S(2)}) async-start(), calls=%async_computation.2 | async-start | bytes 2621440 | tf_op jit(solution)/shard_map/reduce_scatter | solution.py:52
  97.6 0.7 copy-start.3
  97.6 0.7 copy-start.4
  97.7 152.4 %all-reduce.5.cloned.1.call-start = ((), (), s32[]{:S(2)}) async-start(), calls=%async_computation.4 | async-start | bytes 524288 | tf_op jit(solution)/shard_map/psum | solution.py:70
  175.6 2.8 %copy-start.1 = (bf16[512,512]{0,1:T(8,128)(2,1)S(1)}, bf16[512,512]{0,1:T(8,128)(2,1)}, u32[]{:S(2)}) copy-start(bf16[512,512]{0,1:T(8,128)(2,1)} %reduce-scatter.2.cloned.1.call-done) | copy-start | bytes 1572868
  177.1 72.9 %copy-start.2 = (f32[256,512]{1,0:T(8,128)S(1)}, f32[256,512]{1,0:T(8,128)}, u32[]{:S(2)}) copy-start(f32[256,512]{1,0:T(8,128)} %param.8) | copy-start | bytes 1572868
Sparse Core Ops, SparseCore 0:
  12.1 76.0 all-gather.1
  91.8 49.6 all-reduce.2
  144.1 31.4 reduce-scatter.1
  179.4 70.5 all-reduce.4
where the time goes:
time: 259 us; the launch traced here: 258 us
  waiting for transfers between devices  222 us (86%)
  between operations  14 us (5%)
  other arithmetic  7.65 us (3%)
  matrix products  7.36 us (3%)
  local copies, waits for them, and re-layouts  6.81 us (3%)
    all_gather x1, waiting for transfers between devices, per_device(): gathered = lax.all_gather(masked, 'pcol', axis=1, tiled=True)  76.2 us
    psum x1, waiting for transfers between devices, per_device(): lax.psum(quadratic.astype(jnp.bfloat16), 'pcol').astype(jnp.float32)  70.3 us
    psum x1, waiting for transfers between devices, from_root(): return lax.psum(kept, axis)  42.8 us
    reduce_scatter x1, waiting for transfers between devices, per_device(): lax.psum_scatter(product.astype(jnp.bfloat16), 'prow', scatter_dimension=...  33.1 us
    dot_general x1, matrix products, per_device(): product = jnp.dot(ainv, gathered, preferred_element_type=jnp.float32)  5.92 us
  transfers between devices with their start and end apart: 4, of which 4 were waited for; matrix products, arithmetic and copies ran while one was open for 4% of the time, Pallas kernels for 0%

commit v1 on v0

--- a/solution.py
+++ b/solution.py
@@ -1,7 +1,13 @@
+import functools
+
 import jax
 import jax.numpy as jnp
 from jax import lax
+from jax.experimental import pallas as pl
+from jax.experimental.pallas import tpu as pltpu
 from jax.sharding import PartitionSpec as P
+
+MESH = pl.DeviceIdType.MESH
 
 B = 256
 SNODES = 8
@@ -75,10 +81,341 @@
     return (selected_inverse, diagonal_blocks)
 
 
+def level_kernel(
+    n_z, n_x,
+    a_ref, lp_ref, dinv_ref, rb_ref, cnt_ref, wid_ref,
+    sel_ref, diag_ref,
+    a_nb, fbuf, froot, psend, prec, pown, pbf, pnb, dpart, drec, dall,
+    a_sem, fsend, frecv, rsend, rrecv, psend_sem, prec_sem, xsem_s, xsem_r,
+    d1_s, d1_r, d2_s, d2_r,
+):
+    p = lax.axis_index("prow")
+    c = lax.axis_index("pcol")
+    z = lax.div(c, n_x)
+    x = lax.rem(c, n_x)
+    xo = 1 - x
+    rows = a_ref.shape[0]
+    H = 128
+    halves = B // H
+    slots = rb_ref.shape[1]
+    row_blocks = lp_ref.shape[0] // B
+    out_blocks = rows // B
+    slice_rows = B // n_z
+
+    def live(block, node):
+        count = cnt_ref[node]
+        hit = jnp.int32(0)
+        for i in range(slots):
+            hit += jnp.where((rb_ref[node, i] == block) & (i < count), 1, 0)
+        return hit
+
+    def remote(src, dst, s_sem, r_sem, prow, pcol):
+        return pltpu.make_async_remote_copy(
+            src_ref=src, dst_ref=dst, send_sem=s_sem, recv_sem=r_sem,
+            device_id=(prow, pcol), device_id_type=MESH,
+        )
+
+    barrier = pltpu.get_barrier_semaphore()
+    for d in range(1, n_z * n_x):
+        pl.semaphore_signal(barrier, inc=1, device_id=(p, lax.rem(c + d, n_z * n_x)), device_id_type=MESH)
+    for d in range(1, n_z):
+        pl.semaphore_signal(barrier, inc=1, device_id=(lax.rem(p + d, n_z), c), device_id_type=MESH)
+
+    width = wid_ref[c]
+    for b in range(row_blocks):
+        limit = jnp.where(live(p * row_blocks + b, c) > 0, width, 0)
+        for h in range(halves):
+            cols = lax.broadcasted_iota(jnp.int32, (B, H), 1) + h * H
+            value = lp_ref[b * B:(b + 1) * B, h * H:(h + 1) * H].astype(jnp.float32)
+            fbuf[z, h, b * B:(b + 1) * B, :] = jnp.where(cols < limit, value, 0.0).astype(jnp.bfloat16)
+
+    pl.semaphore_wait(barrier, n_z * n_x - 1 + n_z - 1)
+
+    a_copy = remote(a_ref, a_nb, a_sem.at[0], a_sem.at[1], p, z * n_x + xo)
+
+    def f_copy(s, h, way):
+        return remote(
+            fbuf.at[s, h], fbuf.at[s, h], fsend.at[way, s, h], frecv.at[s, h],
+            p, (z + (1 - 2 * way)) * n_x + x,
+        )
+
+    def root_copy(s, h):
+        return remote(fbuf.at[s, h], froot.at[h], rsend.at[s, h], rrecv.at[h], s, c)
+
+    def part_copy(s, r, h):
+        return remote(
+            psend.at[s, r, h], prec.at[p, r, h], psend_sem.at[s, r, h], prec_sem.at[p, r, h], s, c
+        )
+
+    def x_copy(h):
+        return remote(pbf.at[1, h], pnb.at[h], xsem_s.at[h], xsem_r.at[h], p, z * n_x + xo)
+
+    def partial(s, r, h, left):
+        value = jnp.dot(left[...], fbuf[s, h], preferred_element_type=jnp.float32)
+
+        @pl.when(s == p)
+        def _():
+            pown[r, h] = value
+
+        @pl.when(s != p)
+        def _():
+            psend[s, r, h] = value.astype(jnp.bfloat16)
+            part_copy(s, r, h).start()
+
+    def item(i):
+        t = lax.div(i, 2 * halves)
+        h = lax.rem(lax.div(i, 2), halves)
+        way = lax.rem(i, 2)
+        s = z - t * (1 - 2 * way)
+        valid = (s >= 0) & (s < n_z) & ((t > 0) | (way == 0))
+        return t, h, way, s, valid
+
+    def root_send(s, h):
+        @pl.when(p == z)
+        def _():
+            @pl.when(s != z)
+            def _():
+                root_copy(s, h).start()
+
+            @pl.when(s == z)
+            def _():
+                froot[h] = fbuf[s, h]
+
+    for h in range(halves):
+        @pl.when(z < n_z - 1)
+        def _():
+            f_copy(z, h, 0).start()
+
+        @pl.when(z > 0)
+        def _():
+            f_copy(z, h, 1).start()
+
+    a_copy.start()
+
+    def first(i, carry):
+        t, h, way, s, valid = item(i)
+
+        @pl.when(valid)
+        def _():
+            @pl.when(t > 0)
+            def _():
+                f_copy(s, h, way).wait_recv()
+                onward = z + (1 - 2 * way)
+
+                @pl.when((onward >= 0) & (onward < n_z))
+                def _():
+                    f_copy(s, h, way).start()
+
+            root_send(s, h)
+            partial(s, 0, h, a_ref)
+
+        return carry
+
+    early = (n_z - 1) * 2 * halves
+    lax.fori_loop(0, early, first, 0)
+    a_copy.wait_recv()
+
+    def second(i, carry):
+        t, h, way, s, valid = item(i)
+
+        @pl.when(valid)
+        def _():
+            partial(s, 1, h, a_nb)
+
+        return carry
+
+    lax.fori_loop(0, early, second, 0)
+
+    def third(i, carry):
+        t, h, way, s, valid = item(i)
+
+        @pl.when(valid)
+        def _():
+            f_copy(s, h, way).wait_recv()
+            root_send(s, h)
+            partial(s, 0, h, a_ref)
+            partial(s, 1, h, a_nb)
+
+        return carry
+
+    lax.fori_loop(early, early + 2 * halves, third, 0)
+
+    def total(r, h):
+        value = pown[r, h]
+        for d in range(1, n_z):
+            q = lax.rem(p + d, n_z)
+            remote(
+                psend.at[p, r, h], prec.at[q, r, h], psend_sem.at[p, r, h], prec_sem.at[q, r, h], p, c
+            ).wait_recv()
+            value = value + prec[q, r, h].astype(jnp.float32)
+        return value
+
+    signs = [
+        [jnp.where(live(c * out_blocks + b, 2 * p + (x if w == 0 else xo)) > 0, -1.0, 0.0) for b in range(out_blocks)]
+        for w in range(2)
+    ]
+
+    def write(value, w, h):
+        node = x if w == 0 else xo
+        lane = pl.multiple_of(node * B + h * H, H)
+        for b in range(out_blocks):
+            sel_ref[b * B:(b + 1) * B, pl.ds(lane, H)] = (value[b * B:(b + 1) * B] * signs[w][b]).astype(jnp.bfloat16)
+
+    for h in range(halves):
+        pbf[1, h] = total(1, h).astype(jnp.bfloat16)
+        x_copy(h).start()
+        value = total(0, h)
+        pbf[0, h] = value.astype(jnp.bfloat16)
+        write(value, 0, h)
+
+    for h in range(halves):
+        @pl.when(p != z)
+        def _():
+            root_copy(p, h).wait_recv()
+    for h in range(halves):
+        for g in range(halves):
+            value = jnp.zeros((H, H), jnp.float32)
+            for r in range(2):
+                start = pl.multiple_of((x if r == 0 else xo) * rows, rows)
+                value += lax.dot_general(
+                    froot[g, pl.ds(start, rows), :], pbf[r, h], (((0,), (0,)), ((), ())),
+                    preferred_element_type=jnp.float32,
+                )
+            dpart[g * H:(g + 1) * H, h * H:(h + 1) * H] = value.astype(jnp.bfloat16)
+
+    def d1_copy(to, own):
+        return remote(
+            dpart.at[pl.ds(pl.multiple_of(to * slice_rows, slice_rows), slice_rows)], drec.at[own],
+            d1_s.at[to], d1_r.at[own], p, to * n_x + x,
+        )
+
+    for d in range(1, n_z):
+        d1_copy(lax.rem(z + d, n_z), z).start()
+    value = dpart[pl.ds(pl.multiple_of(z * slice_rows, slice_rows), slice_rows)].astype(jnp.float32)
+    for d in range(1, n_z):
+        q = lax.rem(z + d, n_z)
+        d1_copy(q, q).wait_recv()
+        value = value + drec[q].astype(jnp.float32)
+    dall[c] = value.astype(jnp.bfloat16)
+
+    def d2_copy(to, own):
+        return remote(dall.at[own], dall.at[own], d2_s.at[to], d2_r.at[own], p, to)
+
+    for d in range(1, n_z * n_x):
+        d2_copy(lax.rem(c + d, n_z * n_x), c).start()
+
+    for h in range(halves):
+        x_copy(h).wait_recv()
+        write(pnb[h].astype(jnp.float32), 1, h)
+
+    def corner(w, r):
+        wide = wid_ref[2 * p + w]
+        shape = (slice_rows, B)
+        line = lax.broadcasted_iota(jnp.int32, shape, 0) + r * slice_rows
+        col = lax.broadcasted_iota(jnp.int32, shape, 1)
+        own = dinv_ref[r * slice_rows:(r + 1) * slice_rows, w * B:(w + 1) * B]
+        return jnp.where((line < wide) & (col < wide), own, 0.0)
+
+    for d in range(1, n_z * n_x):
+        q = lax.rem(c + d, n_z * n_x)
+        d2_copy(q, q).wait_recv()
+    for r in range(n_z):
+        for w in range(n_x):
+            diag_ref[r * slice_rows:(r + 1) * slice_rows, w * B:(w + 1) * B] = (
+                corner(w, r) + dall[r * n_x + w].astype(jnp.float32)
+            )
+
+    a_copy.wait_send()
+    for h in range(halves):
+        x_copy(h).wait_send()
+    for s in range(n_z):
+        for h in range(halves):
+            @pl.when((s <= z) & (z < n_z - 1))
+            def _():
+                f_copy(s, h, 0).wait_send()
+
+            @pl.when((s >= z) & (z > 0))
+            def _():
+                f_copy(s, h, 1).wait_send()
+
+            @pl.when((p == z) & (s != z))
+            def _():
+                root_copy(s, h).wait_send()
+
+            @pl.when(s != p)
+            def _():
+                for r in range(2):
+                    part_copy(s, r, h).wait_send()
+    for d in range(1, n_z):
+        d1_copy(lax.rem(z + d, n_z), z).wait_send()
+    for d in range(1, n_z * n_x):
+        d2_copy(lax.rem(c + d, n_z * n_x), c).wait_send()
+
+
+def fused(n_prow, n_pcol, ainv, lpanel, dinv, rowblocks, counts, widths):
+    n_z, n_x = n_prow, 2
+    rows, depth = ainv.shape
+    bf, f32, H = jnp.bfloat16, jnp.float32, 128
+    halves = B // H
+    vmem = pl.BlockSpec(memory_space=pltpu.VMEM)
+    smem = pl.BlockSpec(memory_space=pltpu.SMEM)
+    dma = pltpu.SemaphoreType.DMA
+    return pl.pallas_call(
+        functools.partial(level_kernel, n_z, n_x),
+        out_shape=(
+            jax.ShapeDtypeStruct((rows, dinv.shape[1]), bf),
+            jax.ShapeDtypeStruct(dinv.shape, f32),
+        ),
+        in_specs=[vmem] * 3 + [smem] * 3,
+        out_specs=(vmem, vmem),
+        scratch_shapes=[
+            pltpu.VMEM((rows, depth), bf),
+            pltpu.VMEM((n_z, halves, depth, H), bf),
+            pltpu.VMEM((halves, depth, H), bf),
+            pltpu.VMEM((n_z, 2, halves, rows, H), bf),
+            pltpu.VMEM((n_z, 2, halves, rows, H), bf),
+            pltpu.VMEM((2, halves, rows, H), f32),
+            pltpu.VMEM((2, halves, rows, H), bf),
+            pltpu.VMEM((halves, rows, H), bf),
+            pltpu.VMEM((B, B), bf),
+            pltpu.VMEM((n_z, B // n_z, B), bf),
+            pltpu.VMEM((n_z * n_x, B // n_z, B), bf),
+            dma((2,)),
+            dma((2, n_z, halves)),
+            dma((n_z, halves)),
+            dma((n_z, halves)),
+            dma((halves,)),
+            dma((n_z, 2, halves)),
+            dma((n_z, 2, halves)),
+            dma((halves,)),
+            dma((halves,)),
+            dma((n_z,)),
+            dma((n_z,)),
+            dma((n_z * n_x,)),
+            dma((n_z * n_x,)),
+        ],
+        compiler_params=pltpu.CompilerParams(
+            collective_id=0, has_side_effects=True, vmem_limit_bytes=40 * 1024 * 1024
+        ),
+        cost_estimate=pl.CostEstimate(
+            flops=2 * rows * depth * SNODES * B, bytes_accessed=4 * 1024 * 1024, transcendentals=0
+        ),
+    )(ainv, lpanel, dinv, rowblocks, counts, widths)
+
+
 def solution(mesh):
+    n_prow, n_pcol = mesh.shape["prow"], mesh.shape["pcol"]
+
+    def step(ainv, lpanel, dinv, rowblocks, counts, widths):
+        rows, depth = ainv.shape
+        whole = n_pcol == 2 * n_prow and lpanel.shape[1] == B and dinv.shape[1] == 2 * B
+        if whole and depth == 2 * rows and depth == lpanel.shape[0] and rows % B == 0 and B % (16 * n_prow) == 0:
+            return fused(n_prow, n_pcol, ainv, lpanel, dinv, rowblocks, counts, widths)
+        return per_device(ainv, lpanel, dinv, rowblocks, counts, widths)
+
     placed = (P("pcol", "prow"), P("prow", "pcol"), P(None, "prow"), P(), P(), P())
     return jax.shard_map(
-        per_device,
+        step,
         mesh=mesh,
         in_specs=placed,
         out_specs=(P("pcol", "prow"), P(None, "prow")),

time: 259 us -> 75.6 us (0.29)
  waiting for transfers between devices: 222 us -> 0 us
  Pallas kernels: 0 us -> 67.8 us
  between operations: 14 us -> 0.65 us
  other arithmetic: 7.65 us -> 0 us
  matrix products: 7.36 us -> 0 us
    psum x2 -> x0, waiting for transfers between devices: 113 us -> none  [the longest x1 70.3 us: per_device(): lax.psum(quadratic.astype(jnp.bfloat16), 'pcol').astype(jnp.float32)]
    all_gather x1 -> x0, waiting for transfers between devices: 76.2 us -> none  [per_device(): gathered = lax.all_gather(masked, 'pcol', axis=1, tiled=True)]
    pallas_call x0 -> x1, Pallas kernels: none -> 67.8 us  [fused(): pl.pallas_call(functools.partial(level_kernel, n_z, n_x), out_shape=(jax....]
    reduce_scatter x1 -> x0, waiting for transfers between devices: 33.1 us -> none  [per_device(): lax.psum_scatter(product.astype(jnp.bfloat16), 'prow', scatter_dimension=...]
    dot_general x2 -> x0, matrix products: 7.36 us -> none  [the longest x1 5.92 us: per_device(): product = jnp.dot(ainv, gathered, preferred_element_type=jnp.float32)]
    select_n x4 -> x0, other arithmetic: 4.22 us -> none  [the longest x1 3.35 us: from_root(): jnp.where(lax.axis_index(axis) == source, value, 0).astype(value.dtype)]
    unnamed x14, local copies, waits for them, and re-layouts: 3.8 us -> 6.88 us
  transfers between devices with their start and end apart: 4 -> 0, of which waited for: 4 -> 0; matrix products, arithmetic and copies ran while one was open for 4% -> 0% of each run, Pallas kernels for 0% -> 0%
where the time goes in v1:
time: 75.6 us; the launch traced here: 75.3 us
  Pallas kernels  67.8 us (90%)
  local copies, waits for them, and re-layouts  6.88 us (9%)
    pallas_call x1, Pallas kernels, fused(): pl.pallas_call(functools.partial(level_kernel, n_z, n_x), out_shape=(jax....  67.8 us
    unnamed x14, local copies, waits for them, and re-layouts  6.88 us

profile of v1, /device:TPU:0, one launch (start us, length us, event | category | flops | bytes accessed | tf_op | source)
XLA Modules:
  0.0 75.3 jit_solution(6039177182933524415)
XLA Ops:
  0.6 0.0 copy-start
  0.6 1.2 %copy-done = bf16[512,1024]{1,0:T(8,128)(2,1)S(1)} copy-done((bf16[512,1024]{1,0:T(8,128)(2,1)S(1)}, bf16[512,1024]{1,0:T(8,128)(2,1)}, u32[]{:S(2)}) %copy-start) | copy-done | bytes 1048600
  1.9 0.0 copy-start.1
  1.9 1.0 %copy-done.1 = bf16[1024,256]{1,0:T(8,128)(2,1)S(1)} copy-done((bf16[1024,256]{1,0:T(8,128)(2,1)S(1)}, bf16[1024,256]{1,0:T(8,128)(2,1)}, u32[]{:S(2)}) %copy-start.1) | copy-done | bytes 524312
  2.9 0.0 copy-start.2
  2.9 1.0 %copy-done.2 = f32[256,512]{1,0:T(8,128)S(1)} copy-done((f32[256,512]{1,0:T(8,128)S(1)}, f32[256,512]{1,0:T(8,128)}, u32[]{:S(2)}) %copy-start.2) | copy-done | bytes 524312
  3.9 0.0 copy-start.3
  3.9 0.7 copy-done.3
  4.6 0.0 copy-start.4
  4.6 0.7 copy-done.4
  5.3 0.0 copy-start.5
  5.3 0.7 copy-done.5
  5.9 67.8 %shard_map.77 = (bf16[512,512]{1,0:T(8,128)(2,1)S(1)}, f32[256,512]{1,0:T(8,128)S(1)}) custom-call(bf16[512,1024]{1,0:T(8,128)(2,1)S(1)} %copy-done, bf16[1024,256]{1,0:T(8,128)(2,1)S(1)} %copy-done.1, f32[256,512]{1,0:T(8,128)S(1)} %copy-done.2, s32[8,10]{1,0:T(8,128)S(1)} %copy-done.3, s32[8]{0:T(128)S(1)} %copy-done.4, s32[8]{0:T(128)S(1)} %copy-done.5), custom_call_target="tpu_custom_call" | custom-call | flops 2147483648 | bytes 4194304 | tf_op jit(solution)/shard_map/pallas_call | solution.py:363
  73.8 0.8 %copy.10 = bf16[512,512]{1,0:T(8,128)(2,1)} copy(bf16[512,512]{1,0:T(8,128)(2,1)S(1)} %get-tuple-element.4) | data formatting | bytes 1048576
  74.5 0.8 %copy.11 = f32[256,512]{1,0:T(8,128)} copy(f32[256,512]{1,0:T(8,128)S(1)} %get-tuple-element.5) | data formatting | bytes 1048576
Async XLA Ops:
  0.6 1.2 %copy-start = (bf16[512,1024]{1,0:T(8,128)(2,1)S(1)}, bf16[512,1024]{1,0:T(8,128)(2,1)}, u32[]{:S(2)}) copy-start(bf16[512,1024]{1,0:T(8,128)(2,1)} %a_ref.1) | copy-start | bytes 3145732
  1.9 1.0 %copy-start.1 = (bf16[1024,256]{1,0:T(8,128)(2,1)S(1)}, bf16[1024,256]{1,0:T(8,128)(2,1)}, u32[]{:S(2)}) copy-start(bf16[1024,256]{1,0:T(8,128)(2,1)} %lp_ref.1) | copy-start | bytes 1572868
  2.9 1.0 %copy-start.2 = (f32[256,512]{1,0:T(8,128)S(1)}, f32[256,512]{1,0:T(8,128)}, u32[]{:S(2)}) copy-start(f32[256,512]{1,0:T(8,128)} %dinv_ref.1) | copy-start | bytes 1572868
  3.9 0.7 copy-start.3
  4.6 0.7 copy-start.4
  5.3 0.7 copy-start.5

commit v2 on v1

--- a/solution.py
+++ b/solution.py
@@ -83,10 +83,13 @@
 
 def level_kernel(
     n_z, n_x,
-    a_ref, lp_ref, dinv_ref, rb_ref, cnt_ref, wid_ref,
+    a_hbm, lp_hbm, dinv_hbm, rb_hbm, cnt_hbm, wid_hbm,
     sel_ref, diag_ref,
-    a_nb, fbuf, froot, psend, prec, pown, pbf, pnb, dpart, drec, dall,
-    a_sem, fsend, frecv, rsend, rrecv, psend_sem, prec_sem, xsem_s, xsem_r,
+    a_buf, lp_ref, dinv_ref, rb_ref, cnt_ref, wid_ref,
+    fbuf, froot, froot_t, pown, pkeep, pair_out, pair_in, cross_out, cross_in, part_out, part_in,
+    pall, pbf, pnb, dpart, drec, dall,
+    in_sem, a_sem, fsend, frecv, rsend, rrecv,
+    pair_s, pair_r, cross_s, cross_r, part_s, part_r, xsem_s, xsem_r,
     d1_s, d1_r, d2_s, d2_r,
 ):
     p = lax.axis_index("prow")
@@ -94,7 +97,10 @@
     z = lax.div(c, n_x)
     x = lax.rem(c, n_x)
     xo = 1 - x
-    rows = a_ref.shape[0]
+    y = lax.div(p, 2)
+    core = lax.rem(p, 2)
+    mate = 2 * y + 1 - core
+    rows = a_hbm.shape[0]
     H = 128
     halves = B // H
     slots = rb_ref.shape[1]
@@ -102,6 +108,18 @@
     out_blocks = rows // B
     slice_rows = B // n_z
 
+    fetches = [
+        pltpu.make_async_copy(src, dst, in_sem.at[i])
+        for i, (src, dst) in enumerate(
+            [
+                (rb_hbm, rb_ref), (cnt_hbm, cnt_ref), (wid_hbm, wid_ref),
+                (lp_hbm, lp_ref), (a_hbm, a_buf.at[0]), (dinv_hbm, dinv_ref),
+            ]
+        )
+    ]
+    for fetch in fetches:
+        fetch.start()
+
     def live(block, node):
         count = cnt_ref[node]
         hit = jnp.int32(0)
@@ -121,17 +139,7 @@
     for d in range(1, n_z):
         pl.semaphore_signal(barrier, inc=1, device_id=(lax.rem(p + d, n_z), c), device_id_type=MESH)
 
-    width = wid_ref[c]
-    for b in range(row_blocks):
-        limit = jnp.where(live(p * row_blocks + b, c) > 0, width, 0)
-        for h in range(halves):
-            cols = lax.broadcasted_iota(jnp.int32, (B, H), 1) + h * H
-            value = lp_ref[b * B:(b + 1) * B, h * H:(h + 1) * H].astype(jnp.float32)
-            fbuf[z, h, b * B:(b + 1) * B, :] = jnp.where(cols < limit, value, 0.0).astype(jnp.bfloat16)
-
-    pl.semaphore_wait(barrier, n_z * n_x - 1 + n_z - 1)
-
-    a_copy = remote(a_ref, a_nb, a_sem.at[0], a_sem.at[1], p, z * n_x + xo)
+    a_copy = remote(a_hbm, a_buf.at[1], a_sem.at[0], a_sem.at[1], p, z * n_x + xo)
 
     def f_copy(s, h, way):
         return remote(
@@ -142,33 +150,51 @@
     def root_copy(s, h):
         return remote(fbuf.at[s, h], froot.at[h], rsend.at[s, h], rrecv.at[h], s, c)
 
-    def part_copy(s, r, h):
+    def part_copy(r, h):
+        return remote(part_out.at[r, h], part_in.at[r, h], part_s.at[r, h], part_r.at[r, h], mate, c)
+
+    def pair_copy(e, h):
+        return remote(pair_out.at[e, h], pair_in.at[e, h], pair_s.at[e, h], pair_r.at[e, h], mate, c)
+
+    def cross_copy(e, r, h):
         return remote(
-            psend.at[s, r, h], prec.at[p, r, h], psend_sem.at[s, r, h], prec_sem.at[p, r, h], s, c
+            cross_out.at[e, h], cross_in.at[r, h], cross_s.at[e, h], cross_r.at[r, h], 2 * (1 - y) + e, c
         )
 
     def x_copy(h):
-        return remote(pbf.at[1, h], pnb.at[h], xsem_s.at[h], xsem_r.at[h], p, z * n_x + xo)
-
-    def partial(s, r, h, left):
-        value = jnp.dot(left[...], fbuf[s, h], preferred_element_type=jnp.float32)
-
-        @pl.when(s == p)
+        return remote(pbf.at[h], pnb.at[h], xsem_s.at[h], xsem_r.at[h], p, z * n_x + xo)
+
+    def partial(s, r, h):
+        value = jnp.dot(a_buf[r], fbuf[s, h], preferred_element_type=jnp.float32)
+        e = lax.rem(s, 2)
+        same = lax.div(s, 2) == y
+
+        @pl.when(same & (s == p))
         def _():
             pown[r, h] = value
 
-        @pl.when(s != p)
-        def _():
-            psend[s, r, h] = value.astype(jnp.bfloat16)
-            part_copy(s, r, h).start()
-
-    def item(i):
-        t = lax.div(i, 2 * halves)
-        h = lax.rem(lax.div(i, 2), halves)
-        way = lax.rem(i, 2)
-        s = z - t * (1 - 2 * way)
-        valid = (s >= 0) & (s < n_z) & ((t > 0) | (way == 0))
-        return t, h, way, s, valid
+        @pl.when(same & (s != p))
+        def _():
+            part_out[r, h] = value.astype(jnp.bfloat16)
+            part_copy(r, h).start()
+
+        @pl.when(jnp.logical_not(same) & (r == core))
+        def _():
+            pkeep[e, h] = value
+
+        @pl.when(jnp.logical_not(same) & (r != core))
+        def _():
+            pair_out[e, h] = value.astype(jnp.bfloat16)
+            pair_copy(e, h).start()
+
+    def finalize(s, r, h):
+        e = lax.rem(s, 2)
+
+        @pl.when((lax.div(s, 2) != y) & (r == core))
+        def _():
+            pair_copy(e, h).wait_recv()
+            cross_out[e, h] = (pkeep[e, h] + pair_in[e, h].astype(jnp.float32)).astype(jnp.bfloat16)
+            cross_copy(e, r, h).start()
 
     def root_send(s, h):
         @pl.when(p == z)
@@ -181,7 +207,19 @@
             def _():
                 froot[h] = fbuf[s, h]
 
+    for fetch in fetches[:4]:
+        fetch.wait()
+    width = wid_ref[c]
+    limits = [jnp.where(live(p * row_blocks + b, c) > 0, width, 0) for b in range(row_blocks)]
     for h in range(halves):
+        for b in range(row_blocks):
+            cols = lax.broadcasted_iota(jnp.int32, (B, H), 1) + h * H
+            value = lp_ref[b * B:(b + 1) * B, h * H:(h + 1) * H].astype(jnp.float32)
+            fbuf[z, h, b * B:(b + 1) * B, :] = jnp.where(cols < limits[b], value, 0.0).astype(jnp.bfloat16)
+        if h == 0:
+            pl.semaphore_wait(barrier, n_z * n_x - 1 + n_z - 1)
+            a_copy.start()
+
         @pl.when(z < n_z - 1)
         def _():
             f_copy(z, h, 0).start()
@@ -189,66 +227,80 @@
         @pl.when(z > 0)
         def _():
             f_copy(z, h, 1).start()
-
-    a_copy.start()
-
-    def first(i, carry):
-        t, h, way, s, valid = item(i)
-
-        @pl.when(valid)
-        def _():
-            @pl.when(t > 0)
-            def _():
-                f_copy(s, h, way).wait_recv()
-                onward = z + (1 - 2 * way)
-
-                @pl.when((onward >= 0) & (onward < n_z))
-                def _():
-                    f_copy(s, h, way).start()
-
-            root_send(s, h)
-            partial(s, 0, h, a_ref)
-
+    for fetch in fetches[4:]:
+        fetch.wait()
+
+    def both(j, act):
+        t = lax.div(j, halves)
+        h = lax.rem(j, halves)
+        for way in range(2):
+            s = z - t * (1 - 2 * way)
+            valid = (s >= 0) & (s < n_z)
+            if way == 1:
+                valid = valid & (t > 0)
+
+            @pl.when(valid)
+            def _():
+                act(t, h, way, s)
+
+    def arrive(t, h, way, s):
+        @pl.when(t > 0)
+        def _():
+            f_copy(s, h, way).wait_recv()
+            onward = z + (1 - 2 * way)
+
+            @pl.when((onward >= 0) & (onward < n_z))
+            def _():
+                f_copy(s, h, way).start()
+
+        root_send(s, h)
+
+    def first_act(t, h, way, s):
+        arrive(t, h, way, s)
+        partial(s, 0, h)
+
+    def first(j, carry):
+        both(j, first_act)
+        both(j, lambda t, h, way, s: finalize(s, 0, h))
         return carry
 
-    early = (n_z - 1) * 2 * halves
+    early = (n_z - 1) * halves
     lax.fori_loop(0, early, first, 0)
     a_copy.wait_recv()
 
-    def second(i, carry):
-        t, h, way, s, valid = item(i)
-
-        @pl.when(valid)
-        def _():
-            partial(s, 1, h, a_nb)
+    def second(j, carry):
+        @pl.when(j < early)
+        def _():
+            both(j, lambda t, h, way, s: partial(s, 1, h))
+
+        @pl.when(j > 0)
+        def _():
+            both(j - 1, lambda t, h, way, s: finalize(s, 1, h))
 
         return carry
 
-    lax.fori_loop(0, early, second, 0)
-
-    def third(i, carry):
-        t, h, way, s, valid = item(i)
-
-        @pl.when(valid)
-        def _():
-            f_copy(s, h, way).wait_recv()
-            root_send(s, h)
-            partial(s, 0, h, a_ref)
-            partial(s, 1, h, a_nb)
-
+    lax.fori_loop(0, early + 1, second, 0)
+
+    def third_act(t, h, way, s):
+        arrive(t, h, way, s)
+
+        def each(i, carry):
+            partial(s, jnp.where(i == 0, 1 - core, core), h)
+            return carry
+
+        lax.fori_loop(0, 2, each, 0)
+        finalize(s, core, h)
+
+    def third(j, carry):
+        both(j, third_act)
         return carry
 
-    lax.fori_loop(early, early + 2 * halves, third, 0)
+    lax.fori_loop(early, early + halves, third, 0)
 
     def total(r, h):
-        value = pown[r, h]
-        for d in range(1, n_z):
-            q = lax.rem(p + d, n_z)
-            remote(
-                psend.at[p, r, h], prec.at[q, r, h], psend_sem.at[p, r, h], prec_sem.at[q, r, h], p, c
-            ).wait_recv()
-            value = value + prec[q, r, h].astype(jnp.float32)
-        return value
+        part_copy(r, h).wait_recv()
+        cross_copy(core, r, h).wait_recv()
+        return pown[r, h] + part_in[r, h].astype(jnp.float32) + cross_in[r, h].astype(jnp.float32)
 
     signs = [
         [jnp.where(live(c * out_blocks + b, 2 * p + (x if w == 0 else xo)) > 0, -1.0, 0.0) for b in range(out_blocks)]
@@ -262,26 +314,20 @@
             sel_ref[b * B:(b + 1) * B, pl.ds(lane, H)] = (value[b * B:(b + 1) * B] * signs[w][b]).astype(jnp.bfloat16)
 
     for h in range(halves):
-        pbf[1, h] = total(1, h).astype(jnp.bfloat16)
+        @pl.when(p != z)
+        def _():
+            root_copy(p, h).wait_recv()
+        froot_t[h * H:(h + 1) * H, :] = jnp.transpose(froot[h])
+        value = total(1, h).astype(jnp.bfloat16)
+        pbf[h] = value
         x_copy(h).start()
+        pall[pl.ds(pl.multiple_of(xo * rows, rows), rows), h * H:(h + 1) * H] = value
         value = total(0, h)
-        pbf[0, h] = value.astype(jnp.bfloat16)
-        write(value, 0, h)
-
-    for h in range(halves):
-        @pl.when(p != z)
-        def _():
-            root_copy(p, h).wait_recv()
-    for h in range(halves):
-        for g in range(halves):
-            value = jnp.zeros((H, H), jnp.float32)
-            for r in range(2):
-                start = pl.multiple_of((x if r == 0 else xo) * rows, rows)
-                value += lax.dot_general(
-                    froot[g, pl.ds(start, rows), :], pbf[r, h], (((0,), (0,)), ((), ())),
-                    preferred_element_type=jnp.float32,
-                )
-            dpart[g * H:(g + 1) * H, h * H:(h + 1) * H] = value.astype(jnp.bfloat16)
+        pall[pl.ds(pl.multiple_of(x * rows, rows), rows), h * H:(h + 1) * H] = value.astype(jnp.bfloat16)
+        if h < halves - 1:
+            write(value, 0, h)
+
+    dpart[...] = jnp.dot(froot_t[...], pall[...], preferred_element_type=jnp.float32).astype(jnp.bfloat16)
 
     def d1_copy(to, own):
         return remote(
@@ -291,6 +337,7 @@
 
     for d in range(1, n_z):
         d1_copy(lax.rem(z + d, n_z), z).start()
+    write(value, 0, halves - 1)
     value = dpart[pl.ds(pl.multiple_of(z * slice_rows, slice_rows), slice_rows)].astype(jnp.float32)
     for d in range(1, n_z):
         q = lax.rem(z + d, n_z)
@@ -328,6 +375,11 @@
     a_copy.wait_send()
     for h in range(halves):
         x_copy(h).wait_send()
+        for r in range(2):
+            part_copy(r, h).wait_send()
+        for e in range(2):
+            pair_copy(e, h).wait_send()
+            cross_copy(e, core, h).wait_send()
     for s in range(n_z):
         for h in range(halves):
             @pl.when((s <= z) & (z < n_z - 1))
@@ -341,11 +393,6 @@
             @pl.when((p == z) & (s != z))
             def _():
                 root_copy(s, h).wait_send()
-
-            @pl.when(s != p)
-            def _():
-                for r in range(2):
-                    part_copy(s, r, h).wait_send()
     for d in range(1, n_z):
         d1_copy(lax.rem(z + d, n_z), z).wait_send()
     for d in range(1, n_z * n_x):
@@ -358,35 +405,47 @@
     bf, f32, H = jnp.bfloat16, jnp.float32, 128
     halves = B // H
     vmem = pl.BlockSpec(memory_space=pltpu.VMEM)
-    smem = pl.BlockSpec(memory_space=pltpu.SMEM)
+    hbm = pl.BlockSpec(memory_space=pltpu.HBM)
     dma = pltpu.SemaphoreType.DMA
+    piece = (2, halves, rows, H)
     return pl.pallas_call(
         functools.partial(level_kernel, n_z, n_x),
         out_shape=(
             jax.ShapeDtypeStruct((rows, dinv.shape[1]), bf),
             jax.ShapeDtypeStruct(dinv.shape, f32),
         ),
-        in_specs=[vmem] * 3 + [smem] * 3,
+        in_specs=[hbm] * 6,
         out_specs=(vmem, vmem),
         scratch_shapes=[
-            pltpu.VMEM((rows, depth), bf),
+            pltpu.VMEM((2, rows, depth), bf),
+            pltpu.VMEM(lpanel.shape, bf),
+            pltpu.VMEM(dinv.shape, f32),
+            pltpu.SMEM(rowblocks.shape, jnp.int32),
+            pltpu.SMEM(counts.shape, jnp.int32),
+            pltpu.SMEM(widths.shape, jnp.int32),
             pltpu.VMEM((n_z, halves, depth, H), bf),
             pltpu.VMEM((halves, depth, H), bf),
-            pltpu.VMEM((n_z, 2, halves, rows, H), bf),
-            pltpu.VMEM((n_z, 2, halves, rows, H), bf),
-            pltpu.VMEM((2, halves, rows, H), f32),
-            pltpu.VMEM((2, halves, rows, H), bf),
+            pltpu.VMEM((B, depth), bf),
+            pltpu.VMEM(piece, f32),
+            pltpu.VMEM(piece, f32),
+        ]
+        + [pltpu.VMEM(piece, bf)] * 6
+        + [
+            pltpu.VMEM((depth, B), bf),
+            pltpu.VMEM((halves, rows, H), bf),
             pltpu.VMEM((halves, rows, H), bf),
             pltpu.VMEM((B, B), bf),
             pltpu.VMEM((n_z, B // n_z, B), bf),
             pltpu.VMEM((n_z * n_x, B // n_z, B), bf),
+            dma((6,)),
             dma((2,)),
             dma((2, n_z, halves)),
             dma((n_z, halves)),
             dma((n_z, halves)),
             dma((halves,)),
-            dma((n_z, 2, halves)),
-            dma((n_z, 2, halves)),
+        ]
+        + [dma((2, halves))] * 6
+        + [
             dma((halves,)),
             dma((halves,)),
             dma((n_z,)),
@@ -395,7 +454,7 @@
             dma((n_z * n_x,)),
         ],
         compiler_params=pltpu.CompilerParams(
-            collective_id=0, has_side_effects=True, vmem_limit_bytes=40 * 1024 * 1024
+            collective_id=0, has_side_effects=True, vmem_limit_bytes=60 * 1024 * 1024
         ),
         cost_estimate=pl.CostEstimate(
             flops=2 * rows * depth * SNODES * B, bytes_accessed=4 * 1024 * 1024, transcendentals=0
@@ -408,7 +467,7 @@
 
     def step(ainv, lpanel, dinv, rowblocks, counts, widths):
         rows, depth = ainv.shape
-        whole = n_pcol == 2 * n_prow and lpanel.shape[1] == B and dinv.shape[1] == 2 * B
+        whole = n_prow == 4 and n_pcol == 8 and lpanel.shape[1] == B and dinv.shape[1] == 2 * B
         if whole and depth == 2 * rows and depth == lpanel.shape[0] and rows % B == 0 and B % (16 * n_prow) == 0:
             return fused(n_prow, n_pcol, ainv, lpanel, dinv, rowblocks, counts, widths)
         return per_device(ainv, lpanel, dinv, rowblocks, counts, widths)

time: 75.6 us -> 64.1 us (0.85)
  Pallas kernels: 67.8 us -> 60.5 us
  local copies, waits for them, and re-layouts: 6.88 us -> 2.72 us
    pallas_call x1, Pallas kernels: 67.8 us -> 60.5 us  [fused(): pl.pallas_call(functools.partial(level_kernel, n_z, n_x), out_shape=(jax....]
    unnamed x14 -> x4, local copies, waits for them, and re-layouts: 6.88 us -> 2.72 us
where the time goes in v2:
time: 64.1 us; the launch traced here: 63.9 us
  Pallas kernels  60.5 us (94%)
  local copies, waits for them, and re-layouts  2.72 us (4%)
  between operations  0.65 us (1%)
    pallas_call x1, Pallas kernels, fused(): pl.pallas_call(functools.partial(level_kernel, n_z, n_x), out_shape=(jax....  60.5 us
    unnamed x4, local copies, waits for them, and re-layouts  2.72 us

profile of v2, /device:TPU:0, one launch (start us, length us, event | category | flops | bytes accessed | tf_op | source)
XLA Modules:
  0.0 63.9 jit_solution(4188387340190793926)
XLA Ops:
  0.6 60.5 %shard_map.77 = (bf16[512,512]{1,0:T(8,128)(2,1)}, f32[256,512]{1,0:T(8,128)}) custom-call(bf16[512,1024]{1,0:T(8,128)(2,1)} %a_hbm.1, bf16[1024,256]{1,0:T(8,128)(2,1)} %lp_hbm.1, f32[256,512]{1,0:T(8,128)} %dinv_hbm.1, s32[8,10]{1,0:T(8,128)} %rb_hbm.1, s32[8]{0:T(128)} %cnt_hbm.1, s32[8]{0:T(128)} %wid_hbm.1), custom_call_target="tpu_custom_call" | custom-call | flops 2147483648 | bytes 4194304 | tf_op jit(solution)/shard_map/pallas_call | solution.py:411
  61.1 0.0 copy-start
  61.2 1.9 %copy.10 = bf16[512,512]{1,0:T(8,128)(2,1)} copy(bf16[512,512]{1,0:T(8,128)(2,1)} %get-tuple-element.4) | data formatting | bytes 1048576
  63.1 0.0 copy-done
  63.1 0.8 %copy.11 = f32[256,512]{1,0:T(8,128)} copy(f32[256,512]{1,0:T(8,128)S(1)} %copy-done) | data formatting | bytes 1048576
Async XLA Ops:
  61.1 1.9 %copy-start = (f32[256,512]{1,0:T(8,128)S(1)}, f32[256,512]{1,0:T(8,128)}, u32[]{:S(2)}) copy-start(f32[256,512]{1,0:T(8,128)} %get-tuple-element.5) | copy-start | bytes 1572868

commit v3 on v2

--- a/solution.py
+++ b/solution.py
@@ -81,15 +81,29 @@
     return (selected_inverse, diagonal_blocks)
 
 
+PIECES = 4
+
+
+def handoff_kernel(sel_in, diag_in, sel_out, diag_out, sem):
+    copies = []
+    for k, (src, dst) in enumerate([(sel_in, sel_out), (diag_in, diag_out)]):
+        part = src.shape[0] // PIECES
+        for i in range(PIECES):
+            piece = pl.ds(i * part, part)
+            copies.append(pltpu.make_async_copy(src.at[piece], dst.at[piece], sem.at[k * PIECES + i]))
+    for copy in copies:
+        copy.start()
+    for copy in copies:
+        copy.wait()
+
+
 def level_kernel(
     n_z, n_x,
     a_hbm, lp_hbm, dinv_hbm, rb_hbm, cnt_hbm, wid_hbm,
     sel_ref, diag_ref,
     a_buf, lp_ref, dinv_ref, rb_ref, cnt_ref, wid_ref,
-    fbuf, froot, froot_t, pown, pkeep, pair_out, pair_in, cross_out, cross_in, part_out, part_in,
-    pall, pbf, pnb, dpart, drec, dall,
-    in_sem, a_sem, fsend, frecv, rsend, rrecv,
-    pair_s, pair_r, cross_s, cross_r, part_s, part_r, xsem_s, xsem_r,
+    fbuf, f_t, pkeep, pair_out, pair_in, csum, cin, pall, pbf, pnb, dpart, drec, dall,
+    in_sem, a_sem, fsend, frecv, pair_s, pair_r, own_s, root_s, cin_r, xsem_s, xsem_r,
     d1_s, d1_r, d2_s, d2_r,
 ):
     p = lax.axis_index("prow")
@@ -134,10 +148,14 @@
         )
 
     barrier = pltpu.get_barrier_semaphore()
-    for d in range(1, n_z * n_x):
-        pl.semaphore_signal(barrier, inc=1, device_id=(p, lax.rem(c + d, n_z * n_x)), device_id_type=MESH)
-    for d in range(1, n_z):
-        pl.semaphore_signal(barrier, inc=1, device_id=(lax.rem(p + d, n_z), c), device_id_type=MESH)
+    spot = z * n_z + p
+    for d in range(1, n_z * n_z):
+        q = lax.rem(spot + d, n_z * n_z)
+        pl.semaphore_signal(
+            barrier, inc=1, device_id=(lax.rem(q, n_z), lax.div(q, n_z) * n_x + x), device_id_type=MESH
+        )
+    for d in range(n_z):
+        pl.semaphore_signal(barrier, inc=1, device_id=(p, d * n_x + xo), device_id_type=MESH)
 
     a_copy = remote(a_hbm, a_buf.at[1], a_sem.at[0], a_sem.at[1], p, z * n_x + xo)
 
@@ -147,65 +165,45 @@
             p, (z + (1 - 2 * way)) * n_x + x,
         )
 
-    def root_copy(s, h):
-        return remote(fbuf.at[s, h], froot.at[h], rsend.at[s, h], rrecv.at[h], s, c)
-
-    def part_copy(r, h):
-        return remote(part_out.at[r, h], part_in.at[r, h], part_s.at[r, h], part_r.at[r, h], mate, c)
-
-    def pair_copy(e, h):
-        return remote(pair_out.at[e, h], pair_in.at[e, h], pair_s.at[e, h], pair_r.at[e, h], mate, c)
-
-    def cross_copy(e, r, h):
-        return remote(
-            cross_out.at[e, h], cross_in.at[r, h], cross_s.at[e, h], cross_r.at[r, h], 2 * (1 - y) + e, c
-        )
+    def pair_copy(s, h):
+        return remote(pair_out.at[s, h], pair_in.at[s, h], pair_s.at[s, h], pair_r.at[s, h], mate, c)
+
+    def sum_copy(s, h, sem, to):
+        return remote(csum.at[s, h], cin.at[s, y, core, h], sem.at[s, h], cin_r.at[s, y, core, h], to, c)
 
     def x_copy(h):
         return remote(pbf.at[h], pnb.at[h], xsem_s.at[h], xsem_r.at[h], p, z * n_x + xo)
 
     def partial(s, r, h):
         value = jnp.dot(a_buf[r], fbuf[s, h], preferred_element_type=jnp.float32)
-        e = lax.rem(s, 2)
-        same = lax.div(s, 2) == y
-
-        @pl.when(same & (s == p))
-        def _():
-            pown[r, h] = value
-
-        @pl.when(same & (s != p))
-        def _():
-            part_out[r, h] = value.astype(jnp.bfloat16)
-            part_copy(r, h).start()
-
-        @pl.when(jnp.logical_not(same) & (r == core))
-        def _():
-            pkeep[e, h] = value
-
-        @pl.when(jnp.logical_not(same) & (r != core))
-        def _():
-            pair_out[e, h] = value.astype(jnp.bfloat16)
-            pair_copy(e, h).start()
+
+        @pl.when(r == core)
+        def _():
+            pkeep[s, h] = value
+
+        @pl.when(r != core)
+        def _():
+            pair_out[s, h] = value.astype(jnp.bfloat16)
+            pair_copy(s, h).start()
 
     def finalize(s, r, h):
-        e = lax.rem(s, 2)
-
-        @pl.when((lax.div(s, 2) != y) & (r == core))
-        def _():
-            pair_copy(e, h).wait_recv()
-            cross_out[e, h] = (pkeep[e, h] + pair_in[e, h].astype(jnp.float32)).astype(jnp.bfloat16)
-            cross_copy(e, r, h).start()
-
-    def root_send(s, h):
-        @pl.when(p == z)
-        def _():
-            @pl.when(s != z)
-            def _():
-                root_copy(s, h).start()
-
-            @pl.when(s == z)
-            def _():
-                froot[h] = fbuf[s, h]
+        @pl.when(r == core)
+        def _():
+            pair_copy(s, h).wait_recv()
+            value = (pkeep[s, h] + pair_in[s, h].astype(jnp.float32)).astype(jnp.bfloat16)
+            csum[s, h] = value
+
+            @pl.when((s == p) | (z == p))
+            def _():
+                cin[s, y, core, h] = value
+
+            @pl.when((s != z) & (z != p))
+            def _():
+                sum_copy(s, h, root_s, z).start()
+
+            @pl.when(s != p)
+            def _():
+                sum_copy(s, h, own_s, s).start()
 
     for fetch in fetches[:4]:
         fetch.wait()
@@ -217,7 +215,7 @@
             value = lp_ref[b * B:(b + 1) * B, h * H:(h + 1) * H].astype(jnp.float32)
             fbuf[z, h, b * B:(b + 1) * B, :] = jnp.where(cols < limits[b], value, 0.0).astype(jnp.bfloat16)
         if h == 0:
-            pl.semaphore_wait(barrier, n_z * n_x - 1 + n_z - 1)
+            pl.semaphore_wait(barrier, n_z * n_z - 1 + n_z)
             a_copy.start()
 
         @pl.when(z < n_z - 1)
@@ -253,8 +251,6 @@
             def _():
                 f_copy(s, h, way).start()
 
-        root_send(s, h)
-
     def first_act(t, h, way, s):
         arrive(t, h, way, s)
         partial(s, 0, h)
@@ -295,12 +291,37 @@
         both(j, third_act)
         return carry
 
-    lax.fori_loop(early, early + halves, third, 0)
-
-    def total(r, h):
-        part_copy(r, h).wait_recv()
-        cross_copy(core, r, h).wait_recv()
-        return pown[r, h] + part_in[r, h].astype(jnp.float32) + cross_in[r, h].astype(jnp.float32)
+    def total(s, r, h, wait):
+        for g in range(2):
+            @pl.when(wait & (2 * g + r != p))
+            def _():
+                remote(
+                    csum.at[s, h], cin.at[s, g, r, h], own_s.at[s, h], cin_r.at[s, g, r, h], p, c
+                ).wait_recv()
+        return cin[s, 0, r, h].astype(jnp.float32) + cin[s, 1, r, h].astype(jnp.float32)
+
+    def d1_copy(s, to, own):
+        return remote(
+            dpart.at[s, pl.ds(pl.multiple_of(to * slice_rows, slice_rows), slice_rows)], drec.at[own],
+            d1_s.at[s, to], d1_r.at[own], s, to * n_x + x,
+        )
+
+    def diag(s):
+        for h in range(halves):
+            f_t[h * H:(h + 1) * H, :] = jnp.transpose(fbuf[s, h])
+        for h in range(halves):
+            for r in range(2):
+                start = pl.multiple_of((x if r == 0 else xo) * rows, rows)
+                pall[pl.ds(start, rows), h * H:(h + 1) * H] = total(s, r, h, p == z).astype(jnp.bfloat16)
+        dpart[s] = jnp.dot(f_t[...], pall[...], preferred_element_type=jnp.float32).astype(jnp.bfloat16)
+        for to in range(n_z):
+            @pl.when((s == z) & (z == to))
+            def _():
+                drec[z] = dpart[s, to * slice_rows:(to + 1) * slice_rows]
+
+            @pl.when((s != z) | (z != to))
+            def _():
+                d1_copy(s, to, z).start()
 
     signs = [
         [jnp.where(live(c * out_blocks + b, 2 * p + (x if w == 0 else xo)) > 0, -1.0, 0.0) for b in range(out_blocks)]
@@ -313,35 +334,48 @@
         for b in range(out_blocks):
             sel_ref[b * B:(b + 1) * B, pl.ds(lane, H)] = (value[b * B:(b + 1) * B] * signs[w][b]).astype(jnp.bfloat16)
 
-    for h in range(halves):
-        @pl.when(p != z)
-        def _():
-            root_copy(p, h).wait_recv()
-        froot_t[h * H:(h + 1) * H, :] = jnp.transpose(froot[h])
-        value = total(1, h).astype(jnp.bfloat16)
-        pbf[h] = value
-        x_copy(h).start()
-        pall[pl.ds(pl.multiple_of(xo * rows, rows), rows), h * H:(h + 1) * H] = value
-        value = total(0, h)
-        pall[pl.ds(pl.multiple_of(x * rows, rows), rows), h * H:(h + 1) * H] = value.astype(jnp.bfloat16)
-        if h < halves - 1:
-            write(value, 0, h)
-
-    dpart[...] = jnp.dot(froot_t[...], pall[...], preferred_element_type=jnp.float32).astype(jnp.bfloat16)
-
-    def d1_copy(to, own):
-        return remote(
-            dpart.at[pl.ds(pl.multiple_of(to * slice_rows, slice_rows), slice_rows)], drec.at[own],
-            d1_s.at[to], d1_r.at[own], p, to * n_x + x,
-        )
-
-    for d in range(1, n_z):
-        d1_copy(lax.rem(z + d, n_z), z).start()
-    write(value, 0, halves - 1)
-    value = dpart[pl.ds(pl.multiple_of(z * slice_rows, slice_rows), slice_rows)].astype(jnp.float32)
-    for d in range(1, n_z):
-        q = lax.rem(z + d, n_z)
-        d1_copy(q, q).wait_recv()
+    def owner():
+        for h in range(halves):
+            pbf[h] = total(p, 1, h, p != z).astype(jnp.bfloat16)
+            x_copy(h).start()
+            write(total(p, 0, h, p != z), 0, h)
+
+    @pl.when(p == z)
+    def _():
+        def early_diag(i, carry):
+            t = lax.div(i, 2)
+            way = lax.rem(i, 2)
+            s = z - t * (1 - 2 * way)
+
+            @pl.when((s >= 0) & (s < n_z) & ((t > 0) | (way == 0)))
+            def _():
+                diag(s)
+
+            return carry
+
+        lax.fori_loop(0, 2 * (n_z - 1), early_diag, 0)
+
+    last = ((z == 0) & (p == n_z - 1)) | ((z == n_z - 1) & (p == 0))
+
+    @pl.when(jnp.logical_not(last))
+    def _():
+        owner()
+
+    lax.fori_loop(early, early + halves, third, 0)
+
+    @pl.when((p == z) & ((z == 0) | (z == n_z - 1)))
+    def _():
+        diag(n_z - 1 - z)
+
+    @pl.when(last)
+    def _():
+        owner()
+
+    value = jnp.zeros((slice_rows, B), jnp.float32)
+    for q in range(n_z):
+        @pl.when((q != z) | (p != z))
+        def _():
+            d1_copy(q, z, q).wait_recv()
         value = value + drec[q].astype(jnp.float32)
     dall[c] = value.astype(jnp.bfloat16)
 
@@ -375,13 +409,10 @@
     a_copy.wait_send()
     for h in range(halves):
         x_copy(h).wait_send()
-        for r in range(2):
-            part_copy(r, h).wait_send()
-        for e in range(2):
-            pair_copy(e, h).wait_send()
-            cross_copy(e, core, h).wait_send()
     for s in range(n_z):
         for h in range(halves):
+            pair_copy(s, h).wait_send()
+
             @pl.when((s <= z) & (z < n_z - 1))
             def _():
                 f_copy(s, h, 0).wait_send()
@@ -390,11 +421,17 @@
             def _():
                 f_copy(s, h, 1).wait_send()
 
-            @pl.when((p == z) & (s != z))
-            def _():
-                root_copy(s, h).wait_send()
-    for d in range(1, n_z):
-        d1_copy(lax.rem(z + d, n_z), z).wait_send()
+            @pl.when((s != z) & (z != p))
+            def _():
+                sum_copy(s, h, root_s, z).wait_send()
+
+            @pl.when(s != p)
+            def _():
+                sum_copy(s, h, own_s, s).wait_send()
+        for to in range(n_z):
+            @pl.when((p == z) & ((s != z) | (z != to)))
+            def _():
+                d1_copy(s, to, z).wait_send()
     for d in range(1, n_z * n_x):
         d2_copy(lax.rem(c + d, n_z * n_x), c).wait_send()
 
@@ -407,8 +444,8 @@
     vmem = pl.BlockSpec(memory_space=pltpu.VMEM)
     hbm = pl.BlockSpec(memory_space=pltpu.HBM)
     dma = pltpu.SemaphoreType.DMA
-    piece = (2, halves, rows, H)
-    return pl.pallas_call(
+    piece = (n_z, halves, rows, H)
+    results = pl.pallas_call(
         functools.partial(level_kernel, n_z, n_x),
         out_shape=(
             jax.ShapeDtypeStruct((rows, dinv.shape[1]), bf),
@@ -424,31 +461,29 @@
             pltpu.SMEM(counts.shape, jnp.int32),
             pltpu.SMEM(widths.shape, jnp.int32),
             pltpu.VMEM((n_z, halves, depth, H), bf),
-            pltpu.VMEM((halves, depth, H), bf),
             pltpu.VMEM((B, depth), bf),
             pltpu.VMEM(piece, f32),
-            pltpu.VMEM(piece, f32),
-        ]
-        + [pltpu.VMEM(piece, bf)] * 6
-        + [
+            pltpu.VMEM(piece, bf),
+            pltpu.VMEM(piece, bf),
+            pltpu.VMEM(piece, bf),
+            pltpu.VMEM((n_z, 2, 2, halves, rows, H), bf),
             pltpu.VMEM((depth, B), bf),
             pltpu.VMEM((halves, rows, H), bf),
             pltpu.VMEM((halves, rows, H), bf),
-            pltpu.VMEM((B, B), bf),
+            pltpu.VMEM((n_z, B, B), bf),
             pltpu.VMEM((n_z, B // n_z, B), bf),
             pltpu.VMEM((n_z * n_x, B // n_z, B), bf),
             dma((6,)),
             dma((2,)),
             dma((2, n_z, halves)),
             dma((n_z, halves)),
-            dma((n_z, halves)),
-            dma((halves,)),
         ]
-        + [dma((2, halves))] * 6
+        + [dma((n_z, halves))] * 4
         + [
+            dma((n_z, 2, 2, halves)),
             dma((halves,)),
             dma((halves,)),
-            dma((n_z,)),
+            dma((n_z, n_z)),
             dma((n_z,)),
             dma((n_z * n_x,)),
             dma((n_z * n_x,)),
@@ -460,6 +495,15 @@
             flops=2 * rows * depth * SNODES * B, bytes_accessed=4 * 1024 * 1024, transcendentals=0
         ),
     )(ainv, lpanel, dinv, rowblocks, counts, widths)
+    anywhere = pl.BlockSpec(memory_space=pl.ANY)
+    return pl.pallas_call(
+        handoff_kernel,
+        out_shape=tuple(jax.ShapeDtypeStruct(r.shape, r.dtype) for r in results),
+        in_specs=[anywhere] * 2,
+        out_specs=(anywhere, anywhere),
+        scratch_shapes=[dma((2 * PIECES,))],
+        compiler_params=pltpu.CompilerParams(vmem_limit_bytes=60 * 1024 * 1024),
+    )(*results)
 
 
 def solution(mesh):

time: 64.1 us -> 99.4 us (1.55)
  Pallas kernels: 60.5 us -> 98.6 us
  local copies, waits for them, and re-layouts: 2.72 us -> 0 us
    pallas_call x0 -> x1, Pallas kernels: none -> 32.9 us  [fused(): pl.pallas_call(handoff_kernel, out_shape=tuple((jax.ShapeDtypeStruct(r.sh...]
    pallas_call x1, Pallas kernels: 60.5 us -> 65.7 us  [fused(): pl.pallas_call(functools.partial(level_kernel, n_z, n_x), out_shape=(jax....]
    unnamed x4 -> x0, local copies, waits for them, and re-layouts: 2.72 us -> none
where the time goes in v3:
time: 99.4 us; the launch traced here: 99.2 us
  Pallas kernels  98.6 us (99%)
    pallas_call x1, Pallas kernels, fused(): pl.pallas_call(functools.partial(level_kernel, n_z, n_x), out_shape=(jax....  65.7 us
    pallas_call x1, Pallas kernels, fused(): pl.pallas_call(handoff_kernel, out_shape=tuple((jax.ShapeDtypeStruct(r.sh...  32.9 us

profile of v3, /device:TPU:0, one launch (start us, length us, event | category | flops | bytes accessed | tf_op | source)
XLA Modules:
  0.0 99.2 jit_solution(11750382739716390366)
XLA Ops:
  0.6 65.7 %shard_map.77 = (bf16[512,512]{1,0:T(8,128)(2,1)}, f32[256,512]{1,0:T(8,128)}) custom-call(bf16[512,1024]{1,0:T(8,128)(2,1)} %a_hbm.1, bf16[1024,256]{1,0:T(8,128)(2,1)} %lp_hbm.1, f32[256,512]{1,0:T(8,128)} %dinv_hbm.1, s32[8,10]{1,0:T(8,128)} %rb_hbm.1, s32[8]{0:T(128)} %cnt_hbm.1, s32[8]{0:T(128)} %wid_hbm.1), custom_call_target="tpu_custom_call" | custom-call | flops 2147483648 | bytes 4194304 | tf_op jit(solution)/shard_map/pallas_call | solution.py:448
  66.3 32.9 %shard_map.78 = (bf16[512,512]{1,0:T(8,128)(2,1)}, f32[256,512]{1,0:T(8,128)}) custom-call(bf16[512,512]{1,0:T(8,128)(2,1)} %get-tuple-element.4.sel_in, f32[256,512]{1,0:T(8,128)} %get-tuple-element.5.diag_in), custom_call_target="tpu_custom_call" | custom-call | tf_op jit(solution)/shard_map/pallas_call | solution.py:499

commit v4 on v2

--- a/solution.py
+++ b/solution.py
@@ -81,6 +81,27 @@
     return (selected_inverse, diagonal_blocks)
 
 
+PIECES = 2
+
+
+def handoff_kernel(sel_in, diag_in, sel_out, diag_out, sel_held, diag_held, in_sem, out_sem):
+    reads, writes = [], []
+    for k, (src, held, dst) in enumerate([(sel_in, sel_held, sel_out), (diag_in, diag_held, diag_out)]):
+        part = src.shape[0] // PIECES
+        for i in range(PIECES):
+            piece = pl.ds(i * part, part)
+            n = k * PIECES + i
+            reads.append(pltpu.make_async_copy(src.at[piece], held.at[piece], in_sem.at[n]))
+            writes.append(pltpu.make_async_copy(held.at[piece], dst.at[piece], out_sem.at[n]))
+    for copy in reads:
+        copy.start()
+    for read, write in zip(reads, writes):
+        read.wait()
+        write.start()
+    for copy in writes:
+        copy.wait()
+
+
 def level_kernel(
     n_z, n_x,
     a_hbm, lp_hbm, dinv_hbm, rb_hbm, cnt_hbm, wid_hbm,
@@ -88,9 +109,10 @@
     a_buf, lp_ref, dinv_ref, rb_ref, cnt_ref, wid_ref,
     fbuf, froot, froot_t, pown, pkeep, pair_out, pair_in, cross_out, cross_in, part_out, part_in,
     pall, pbf, pnb, dpart, drec, dall,
+    late_keep, late_out, late_in, late_sum, late_cin, late_dpart,
     in_sem, a_sem, fsend, frecv, rsend, rrecv,
     pair_s, pair_r, cross_s, cross_r, part_s, part_r, xsem_s, xsem_r,
-    d1_s, d1_r, d2_s, d2_r,
+    d1_s, d1_r, d2_s, d2_r, late_ps, late_pr, late_ss, late_cr, late_ds,
 ):
     p = lax.axis_index("prow")
     c = lax.axis_index("pcol")
@@ -134,10 +156,14 @@
         )
 
     barrier = pltpu.get_barrier_semaphore()
-    for d in range(1, n_z * n_x):
-        pl.semaphore_signal(barrier, inc=1, device_id=(p, lax.rem(c + d, n_z * n_x)), device_id_type=MESH)
-    for d in range(1, n_z):
-        pl.semaphore_signal(barrier, inc=1, device_id=(lax.rem(p + d, n_z), c), device_id_type=MESH)
+    spot = z * n_z + p
+    for d in range(1, n_z * n_z):
+        q = lax.rem(spot + d, n_z * n_z)
+        pl.semaphore_signal(
+            barrier, inc=1, device_id=(lax.rem(q, n_z), lax.div(q, n_z) * n_x + x), device_id_type=MESH
+        )
+    for d in range(n_z):
+        pl.semaphore_signal(barrier, inc=1, device_id=(p, d * n_x + xo), device_id_type=MESH)
 
     a_copy = remote(a_hbm, a_buf.at[1], a_sem.at[0], a_sem.at[1], p, z * n_x + xo)
 
@@ -217,7 +243,7 @@
             value = lp_ref[b * B:(b + 1) * B, h * H:(h + 1) * H].astype(jnp.float32)
             fbuf[z, h, b * B:(b + 1) * B, :] = jnp.where(cols < limits[b], value, 0.0).astype(jnp.bfloat16)
         if h == 0:
-            pl.semaphore_wait(barrier, n_z * n_x - 1 + n_z - 1)
+            pl.semaphore_wait(barrier, n_z * n_z - 1 + n_z)
             a_copy.start()
 
         @pl.when(z < n_z - 1)
@@ -253,19 +279,27 @@
             def _():
                 f_copy(s, h, way).start()
 
-        root_send(s, h)
-
-    def first_act(t, h, way, s):
-        arrive(t, h, way, s)
-        partial(s, 0, h)
+        @pl.when(t < n_z - 1)
+        def _():
+            root_send(s, h)
 
     def first(j, carry):
-        both(j, first_act)
-        both(j, lambda t, h, way, s: finalize(s, 0, h))
+        @pl.when(j < early)
+        def _():
+            both(j, arrive)
+
+        @pl.when(j > 0)
+        def _():
+            both(j - 1, lambda t, h, way, s: finalize(s, 0, h))
+
+        @pl.when(j < early)
+        def _():
+            both(j, lambda t, h, way, s: partial(s, 0, h))
+
         return carry
 
     early = (n_z - 1) * halves
-    lax.fori_loop(0, early, first, 0)
+    lax.fori_loop(0, early + 1, first, 0)
     a_copy.wait_recv()
 
     def second(j, carry):
@@ -281,15 +315,59 @@
 
     lax.fori_loop(0, early + 1, second, 0)
 
+    late = n_z - 1 - z
+    at_end = (z == 0) | (z == n_z - 1)
+    late_owner = at_end & (p == late)
+    late_root = at_end & (p == z)
+
+    def late_pair(h):
+        return remote(late_out.at[h], late_in.at[h], late_ps.at[h], late_pr.at[h], mate, c)
+
+    def late_copy(h, i, to):
+        return remote(late_sum.at[h], late_cin.at[y, core, h], late_ss.at[i, h], late_cr.at[y, core, h], to, c)
+
     def third_act(t, h, way, s):
         arrive(t, h, way, s)
 
         def each(i, carry):
-            partial(s, jnp.where(i == 0, 1 - core, core), h)
+            value = jnp.dot(a_buf[jnp.where(i == 0, 1 - core, core)], fbuf[s, h], preferred_element_type=jnp.float32)
+
+            @pl.when(i == 0)
+            def _():
+                late_out[h] = value.astype(jnp.bfloat16)
+                late_pair(h).start()
+
+            @pl.when(i == 1)
+            def _():
+                late_keep[h] = value
+
             return carry
 
         lax.fori_loop(0, 2, each, 0)
-        finalize(s, core, h)
+        late_pair(h).wait_recv()
+        value = (late_keep[h] + late_in[h].astype(jnp.float32)).astype(jnp.bfloat16)
+        late_sum[h] = value
+
+        @pl.when((p == z) | (p == late))
+        def _():
+            late_cin[y, core, h] = value
+
+        @pl.when(p != z)
+        def _():
+            late_copy(h, 0, z).start()
+
+        @pl.when(p != late)
+        def _():
+            late_copy(h, 1, late).start()
+
+    def late_total(r, h):
+        for g in range(2):
+            @pl.when(2 * g + r != p)
+            def _():
+                remote(
+                    late_sum.at[h], late_cin.at[g, r, h], late_ss.at[0, h], late_cr.at[g, r, h], p, c
+                ).wait_recv()
+        return late_cin[0, r, h].astype(jnp.float32) + late_cin[1, r, h].astype(jnp.float32)
 
     def third(j, carry):
         both(j, third_act)
@@ -313,21 +391,7 @@
         for b in range(out_blocks):
             sel_ref[b * B:(b + 1) * B, pl.ds(lane, H)] = (value[b * B:(b + 1) * B] * signs[w][b]).astype(jnp.bfloat16)
 
-    for h in range(halves):
-        @pl.when(p != z)
-        def _():
-            root_copy(p, h).wait_recv()
-        froot_t[h * H:(h + 1) * H, :] = jnp.transpose(froot[h])
-        value = total(1, h).astype(jnp.bfloat16)
-        pbf[h] = value
-        x_copy(h).start()
-        pall[pl.ds(pl.multiple_of(xo * rows, rows), rows), h * H:(h + 1) * H] = value
-        value = total(0, h)
-        pall[pl.ds(pl.multiple_of(x * rows, rows), rows), h * H:(h + 1) * H] = value.astype(jnp.bfloat16)
-        if h < halves - 1:
-            write(value, 0, h)
-
-    dpart[...] = jnp.dot(froot_t[...], pall[...], preferred_element_type=jnp.float32).astype(jnp.bfloat16)
+    starts = [pl.multiple_of(x * rows, rows), pl.multiple_of(xo * rows, rows)]
 
     def d1_copy(to, own):
         return remote(
@@ -335,13 +399,56 @@
             d1_s.at[to], d1_r.at[own], p, to * n_x + x,
         )
 
-    for d in range(1, n_z):
-        d1_copy(lax.rem(z + d, n_z), z).start()
-    write(value, 0, halves - 1)
-    value = dpart[pl.ds(pl.multiple_of(z * slice_rows, slice_rows), slice_rows)].astype(jnp.float32)
-    for d in range(1, n_z):
-        q = lax.rem(z + d, n_z)
-        d1_copy(q, q).wait_recv()
+    def late_d1(to):
+        return remote(
+            late_dpart.at[to * slice_rows:(to + 1) * slice_rows], drec.at[z],
+            late_ds.at[to], d1_r.at[z], late, to * n_x + x,
+        )
+
+    @pl.when(jnp.logical_not(late_owner))
+    def _():
+        for h in range(halves):
+            @pl.when(p != z)
+            def _():
+                root_copy(p, h).wait_recv()
+            froot_t[h * H:(h + 1) * H, :] = jnp.transpose(froot[h])
+            value = total(1, h).astype(jnp.bfloat16)
+            pbf[h] = value
+            x_copy(h).start()
+            pall[pl.ds(starts[1], rows), h * H:(h + 1) * H] = value
+            value = total(0, h)
+            pall[pl.ds(starts[0], rows), h * H:(h + 1) * H] = value.astype(jnp.bfloat16)
+            write(value, 0, h)
+        dpart[...] = jnp.dot(froot_t[...], pall[...], preferred_element_type=jnp.float32).astype(jnp.bfloat16)
+        drec[z] = dpart[pl.ds(pl.multiple_of(z * slice_rows, slice_rows), slice_rows)]
+        for d in range(1, n_z):
+            d1_copy(lax.rem(z + d, n_z), z).start()
+
+    @pl.when(late_owner)
+    def _():
+        for h in range(halves):
+            pbf[h] = late_total(1, h).astype(jnp.bfloat16)
+            x_copy(h).start()
+            write(late_total(0, h), 0, h)
+
+    @pl.when(late_root)
+    def _():
+        for h in range(halves):
+            froot_t[h * H:(h + 1) * H, :] = jnp.transpose(fbuf[late, h])
+        for h in range(halves):
+            for r in range(2):
+                pall[pl.ds(starts[r], rows), h * H:(h + 1) * H] = late_total(r, h).astype(jnp.bfloat16)
+        late_dpart[...] = jnp.dot(
+            froot_t[...], pall[...], preferred_element_type=jnp.float32
+        ).astype(jnp.bfloat16)
+        for to in range(n_z):
+            late_d1(to).start()
+
+    value = jnp.zeros((slice_rows, B), jnp.float32)
+    for q in range(n_z):
+        @pl.when((q != z) | late_owner)
+        def _():
+            d1_copy(q, q).wait_recv()
         value = value + drec[q].astype(jnp.float32)
     dall[c] = value.astype(jnp.bfloat16)
 
@@ -375,12 +482,20 @@
     a_copy.wait_send()
     for h in range(halves):
         x_copy(h).wait_send()
-        for r in range(2):
-            part_copy(r, h).wait_send()
-        for e in range(2):
-            pair_copy(e, h).wait_send()
-            cross_copy(e, core, h).wait_send()
+        @pl.when(at_end)
+        def _():
+            late_pair(h).wait_send()
+
+            @pl.when(p != z)
+            def _():
+                late_copy(h, 0, z).wait_send()
+
+            @pl.when(p != late)
+            def _():
+                late_copy(h, 1, late).wait_send()
+
     for s in range(n_z):
+        off = (s == late) & at_end
         for h in range(halves):
             @pl.when((s <= z) & (z < n_z - 1))
             def _():
@@ -390,11 +505,29 @@
             def _():
                 f_copy(s, h, 1).wait_send()
 
-            @pl.when((p == z) & (s != z))
+            @pl.when((p == z) & (s != z) & jnp.logical_not(off))
             def _():
                 root_copy(s, h).wait_send()
-    for d in range(1, n_z):
-        d1_copy(lax.rem(z + d, n_z), z).wait_send()
+
+            @pl.when(jnp.logical_not(off) & (s == mate))
+            def _():
+                for r in range(2):
+                    part_copy(r, h).wait_send()
+
+            @pl.when(jnp.logical_not(off) & (lax.div(jnp.int32(s), 2) != y))
+            def _():
+                pair_copy(s % 2, h).wait_send()
+                cross_copy(s % 2, core, h).wait_send()
+
+    @pl.when(jnp.logical_not(late_owner))
+    def _():
+        for d in range(1, n_z):
+            d1_copy(lax.rem(z + d, n_z), z).wait_send()
+
+    @pl.when(late_root)
+    def _():
+        for to in range(n_z):
+            late_d1(to).wait_send()
     for d in range(1, n_z * n_x):
         d2_copy(lax.rem(c + d, n_z * n_x), c).wait_send()
 
@@ -408,7 +541,7 @@
     hbm = pl.BlockSpec(memory_space=pltpu.HBM)
     dma = pltpu.SemaphoreType.DMA
     piece = (2, halves, rows, H)
-    return pl.pallas_call(
+    results = pl.pallas_call(
         functools.partial(level_kernel, n_z, n_x),
         out_shape=(
             jax.ShapeDtypeStruct((rows, dinv.shape[1]), bf),
@@ -437,6 +570,12 @@
             pltpu.VMEM((B, B), bf),
             pltpu.VMEM((n_z, B // n_z, B), bf),
             pltpu.VMEM((n_z * n_x, B // n_z, B), bf),
+            pltpu.VMEM((halves, rows, H), f32),
+            pltpu.VMEM((halves, rows, H), bf),
+            pltpu.VMEM((halves, rows, H), bf),
+            pltpu.VMEM((halves, rows, H), bf),
+            pltpu.VMEM((2, 2, halves, rows, H), bf),
+            pltpu.VMEM((B, B), bf),
             dma((6,)),
             dma((2,)),
             dma((2, n_z, halves)),
@@ -452,6 +591,11 @@
             dma((n_z,)),
             dma((n_z * n_x,)),
             dma((n_z * n_x,)),
+            dma((halves,)),
+            dma((halves,)),
+            dma((2, halves)),
+            dma((2, 2, halves)),
+            dma((n_z,)),
         ],
         compiler_params=pltpu.CompilerParams(
             collective_id=0, has_side_effects=True, vmem_limit_bytes=60 * 1024 * 1024
@@ -460,6 +604,16 @@
             flops=2 * rows * depth * SNODES * B, bytes_accessed=4 * 1024 * 1024, transcendentals=0
         ),
     )(ainv, lpanel, dinv, rowblocks, counts, widths)
+    anywhere = pl.BlockSpec(memory_space=pl.ANY)
+    return pl.pallas_call(
+        handoff_kernel,
+        out_shape=tuple(jax.ShapeDtypeStruct(r.shape, r.dtype) for r in results),
+        in_specs=[anywhere] * 2,
+        out_specs=(anywhere, anywhere),
+        scratch_shapes=[pltpu.VMEM(r.shape, r.dtype) for r in results]
+        + [dma((2 * PIECES,)), dma((2 * PIECES,))],
+        compiler_params=pltpu.CompilerParams(vmem_limit_bytes=60 * 1024 * 1024),
+    )(*results)
 
 
 def solution(mesh):

time: 64.1 us -> 61.7 us (0.963)
  local copies, waits for them, and re-layouts: 2.72 us -> 0 us
    unnamed x4 -> x0, local copies, waits for them, and re-layouts: 2.72 us -> none
    pallas_call x0 -> x1, Pallas kernels: none -> 1.98 us  [fused(): pl.pallas_call(handoff_kernel, out_shape=tuple((jax.ShapeDtypeStruct(r.sh...]
    pallas_call x1, Pallas kernels: 60.5 us -> 58.9 us  [fused(): pl.pallas_call(functools.partial(level_kernel, n_z, n_x), out_shape=(jax....]
where the time goes in v4:
time: 61.7 us; the launch traced here: 61.5 us
  Pallas kernels  60.9 us (99%)
  between operations  0.64 us (1%)
    pallas_call x1, Pallas kernels, fused(): pl.pallas_call(functools.partial(level_kernel, n_z, n_x), out_shape=(jax....  58.9 us
    pallas_call x1, Pallas kernels, fused(): pl.pallas_call(handoff_kernel, out_shape=tuple((jax.ShapeDtypeStruct(r.sh...  1.98 us

profile of v4, /device:TPU:0, one launch (start us, length us, event | category | flops | bytes accessed | tf_op | source)
XLA Modules:
  0.0 61.5 jit_solution(5247057392455126933)
XLA Ops:
  0.6 58.9 %shard_map.77 = (bf16[512,512]{1,0:T(8,128)(2,1)}, f32[256,512]{1,0:T(8,128)}) custom-call(bf16[512,1024]{1,0:T(8,128)(2,1)} %a_hbm.1, bf16[1024,256]{1,0:T(8,128)(2,1)} %lp_hbm.1, f32[256,512]{1,0:T(8,128)} %dinv_hbm.1, s32[8,10]{1,0:T(8,128)} %rb_hbm.1, s32[8]{0:T(128)} %cnt_hbm.1, s32[8]{0:T(128)} %wid_hbm.1), custom_call_target="tpu_custom_call" | custom-call | flops 2147483648 | bytes 4194304 | tf_op jit(solution)/shard_map/pallas_call | solution.py:544
  59.5 2.0 %shard_map.78 = (bf16[512,512]{1,0:T(8,128)(2,1)}, f32[256,512]{1,0:T(8,128)}) custom-call(bf16[512,512]{1,0:T(8,128)(2,1)} %get-tuple-element.4.sel_in, f32[256,512]{1,0:T(8,128)} %get-tuple-element.5.diag_in), custom_call_target="tpu_custom_call" | custom-call | tf_op jit(solution)/shard_map/pallas_call | solution.py:608

commit v5 on v4

--- a/solution.py
+++ b/solution.py
@@ -105,14 +105,14 @@
 def level_kernel(
     n_z, n_x,
     a_hbm, lp_hbm, dinv_hbm, rb_hbm, cnt_hbm, wid_hbm,
-    sel_ref, diag_ref,
-    a_buf, lp_ref, dinv_ref, rb_ref, cnt_ref, wid_ref,
+    sel_hbm, diag_hbm,
+    sel_ref, diag_ref, a_buf, lp_ref, dinv_ref, rb_ref, cnt_ref, wid_ref,
     fbuf, froot, froot_t, pown, pkeep, pair_out, pair_in, cross_out, cross_in, part_out, part_in,
     pall, pbf, pnb, dpart, drec, dall,
     late_keep, late_out, late_in, late_sum, late_cin, late_dpart,
     in_sem, a_sem, fsend, frecv, rsend, rrecv,
     pair_s, pair_r, cross_s, cross_r, part_s, part_r, xsem_s, xsem_r,
-    d1_s, d1_r, d2_s, d2_r, late_ps, late_pr, late_ss, late_cr, late_ds,
+    d1_s, d1_r, d2_s, d2_r, late_ps, late_pr, late_ss, late_cr, late_ds, out_s,
 ):
     p = lax.axis_index("prow")
     c = lax.axis_index("pcol")
@@ -300,85 +300,9 @@
 
     early = (n_z - 1) * halves
     lax.fori_loop(0, early + 1, first, 0)
-    a_copy.wait_recv()
-
-    def second(j, carry):
-        @pl.when(j < early)
-        def _():
-            both(j, lambda t, h, way, s: partial(s, 1, h))
-
-        @pl.when(j > 0)
-        def _():
-            both(j - 1, lambda t, h, way, s: finalize(s, 1, h))
-
-        return carry
-
-    lax.fori_loop(0, early + 1, second, 0)
-
-    late = n_z - 1 - z
-    at_end = (z == 0) | (z == n_z - 1)
-    late_owner = at_end & (p == late)
-    late_root = at_end & (p == z)
-
-    def late_pair(h):
-        return remote(late_out.at[h], late_in.at[h], late_ps.at[h], late_pr.at[h], mate, c)
-
-    def late_copy(h, i, to):
-        return remote(late_sum.at[h], late_cin.at[y, core, h], late_ss.at[i, h], late_cr.at[y, core, h], to, c)
-
-    def third_act(t, h, way, s):
-        arrive(t, h, way, s)
-
-        def each(i, carry):
-            value = jnp.dot(a_buf[jnp.where(i == 0, 1 - core, core)], fbuf[s, h], preferred_element_type=jnp.float32)
-
-            @pl.when(i == 0)
-            def _():
-                late_out[h] = value.astype(jnp.bfloat16)
-                late_pair(h).start()
-
-            @pl.when(i == 1)
-            def _():
-                late_keep[h] = value
-
-            return carry
-
-        lax.fori_loop(0, 2, each, 0)
-        late_pair(h).wait_recv()
-        value = (late_keep[h] + late_in[h].astype(jnp.float32)).astype(jnp.bfloat16)
-        late_sum[h] = value
-
-        @pl.when((p == z) | (p == late))
-        def _():
-            late_cin[y, core, h] = value
-
-        @pl.when(p != z)
-        def _():
-            late_copy(h, 0, z).start()
-
-        @pl.when(p != late)
-        def _():
-            late_copy(h, 1, late).start()
-
-    def late_total(r, h):
-        for g in range(2):
-            @pl.when(2 * g + r != p)
-            def _():
-                remote(
-                    late_sum.at[h], late_cin.at[g, r, h], late_ss.at[0, h], late_cr.at[g, r, h], p, c
-                ).wait_recv()
-        return late_cin[0, r, h].astype(jnp.float32) + late_cin[1, r, h].astype(jnp.float32)
-
-    def third(j, carry):
-        both(j, third_act)
-        return carry
-
-    lax.fori_loop(early, early + halves, third, 0)
-
-    def total(r, h):
-        part_copy(r, h).wait_recv()
-        cross_copy(core, r, h).wait_recv()
-        return pown[r, h] + part_in[r, h].astype(jnp.float32) + cross_in[r, h].astype(jnp.float32)
+    def sel_copy(w, h):
+        lane = pl.multiple_of((x if w == 0 else xo) * B + h * H, H)
+        return pltpu.make_async_copy(sel_ref.at[:, pl.ds(lane, H)], sel_hbm.at[:, pl.ds(lane, H)], out_s.at[w, h])
 
     signs = [
         [jnp.where(live(c * out_blocks + b, 2 * p + (x if w == 0 else xo)) > 0, -1.0, 0.0) for b in range(out_blocks)]
@@ -390,20 +314,133 @@
         lane = pl.multiple_of(node * B + h * H, H)
         for b in range(out_blocks):
             sel_ref[b * B:(b + 1) * B, pl.ds(lane, H)] = (value[b * B:(b + 1) * B] * signs[w][b]).astype(jnp.bfloat16)
+        sel_copy(w, h).start()
+
+    def corner(w, r):
+        wide = wid_ref[2 * p + w]
+        shape = (slice_rows, B)
+        line = lax.broadcasted_iota(jnp.int32, shape, 0) + r * slice_rows
+        col = lax.broadcasted_iota(jnp.int32, shape, 1)
+        own = dinv_ref[r * slice_rows:(r + 1) * slice_rows, w * B:(w + 1) * B]
+        return jnp.where((line < wide) & (col < wide), own, 0.0)
+
+    for r in range(n_z):
+        for w in range(n_x):
+            diag_ref[r * slice_rows:(r + 1) * slice_rows, w * B:(w + 1) * B] = corner(w, r)
+    a_copy.wait_recv()
+
+    def second(j, carry):
+        @pl.when(j < early)
+        def _():
+            both(j, lambda t, h, way, s: partial(s, 1, h))
+
+        @pl.when(j > 0)
+        def _():
+            both(j - 1, lambda t, h, way, s: finalize(s, 1, h))
+
+        return carry
+
+    lax.fori_loop(0, early + 1, second, 0)
+
+    late = n_z - 1 - z
+    at_end = (z == 0) | (z == n_z - 1)
+    late_owner = at_end & (p == late)
+    late_root = at_end & (p == z)
+
+    def late_pair(h):
+        return remote(late_out.at[h], late_in.at[h], late_ps.at[h], late_pr.at[h], mate, c)
+
+    def late_copy(h, i, to):
+        return remote(late_sum.at[h], late_cin.at[y, core, h], late_ss.at[i, h], late_cr.at[y, core, h], to, c)
+
+    def third_act(t, h, way, s):
+        arrive(t, h, way, s)
+
+        def each(i, carry):
+            value = jnp.dot(a_buf[jnp.where(i == 0, 1 - core, core)], fbuf[s, h], preferred_element_type=jnp.float32)
+
+            @pl.when(i == 0)
+            def _():
+                late_out[h] = value.astype(jnp.bfloat16)
+                late_pair(h).start()
+
+            @pl.when(i == 1)
+            def _():
+                late_keep[h] = value
+
+            return carry
+
+        lax.fori_loop(0, 2, each, 0)
+        late_pair(h).wait_recv()
+        value = (late_keep[h] + late_in[h].astype(jnp.float32)).astype(jnp.bfloat16)
+        late_sum[h] = value
+
+        @pl.when((p == z) | (p == late))
+        def _():
+            late_cin[y, core, h] = value
+
+        @pl.when(p != z)
+        def _():
+            late_copy(h, 0, z).start()
+
+        @pl.when(p != late)
+        def _():
+            late_copy(h, 1, late).start()
+
+    def late_total(r, h):
+        for g in range(2):
+            @pl.when(2 * g + r != p)
+            def _():
+                remote(
+                    late_sum.at[h], late_cin.at[g, r, h], late_ss.at[0, h], late_cr.at[g, r, h], p, c
+                ).wait_recv()
+        return late_cin[0, r, h].astype(jnp.float32) + late_cin[1, r, h].astype(jnp.float32)
+
+    def third(j, carry):
+        both(j, third_act)
+        return carry
+
+    lax.fori_loop(early, early + halves, third, 0)
+
+    def total(r, h):
+        part_copy(r, h).wait_recv()
+        cross_copy(core, r, h).wait_recv()
+        return pown[r, h] + part_in[r, h].astype(jnp.float32) + cross_in[r, h].astype(jnp.float32)
 
     starts = [pl.multiple_of(x * rows, rows), pl.multiple_of(xo * rows, rows)]
 
-    def d1_copy(to, own):
+    def d1_copy(to, own, h):
         return remote(
-            dpart.at[pl.ds(pl.multiple_of(to * slice_rows, slice_rows), slice_rows)], drec.at[own],
-            d1_s.at[to], d1_r.at[own], p, to * n_x + x,
+            dpart.at[h, pl.ds(pl.multiple_of(to * slice_rows, slice_rows), slice_rows)], drec.at[own, h],
+            d1_s.at[to, h], d1_r.at[own, h], p, to * n_x + x,
         )
 
-    def late_d1(to):
+    def late_d1(to, h):
         return remote(
-            late_dpart.at[to * slice_rows:(to + 1) * slice_rows], drec.at[z],
-            late_ds.at[to], d1_r.at[z], late, to * n_x + x,
+            late_dpart.at[h, to * slice_rows:(to + 1) * slice_rows], drec.at[z, h],
+            late_ds.at[to, h], d1_r.at[z, h], late, to * n_x + x,
         )
+
+    def diag_half(out, h):
+        out[h] = jnp.dot(
+            froot_t[...], pall[:, h * H:(h + 1) * H], preferred_element_type=jnp.float32
+        ).astype(jnp.bfloat16)
+
+    def late_half(h):
+        @pl.when(late_root)
+        def _():
+            for r in range(2):
+                pall[pl.ds(starts[r], rows), h * H:(h + 1) * H] = late_total(r, h).astype(jnp.bfloat16)
+            diag_half(late_dpart, h)
+            for to in range(n_z):
+                late_d1(to, h).start()
+
+    @pl.when(late_root)
+    def _():
+        for h in range(halves):
+            froot_t[h * H:(h + 1) * H, :] = jnp.transpose(fbuf[late, h])
+
+    late_half(0)
 
     @pl.when(jnp.logical_not(late_owner))
     def _():
@@ -419,10 +456,11 @@
             value = total(0, h)
             pall[pl.ds(starts[0], rows), h * H:(h + 1) * H] = value.astype(jnp.bfloat16)
             write(value, 0, h)
-        dpart[...] = jnp.dot(froot_t[...], pall[...], preferred_element_type=jnp.float32).astype(jnp.bfloat16)
-        drec[z] = dpart[pl.ds(pl.multiple_of(z * slice_rows, slice_rows), slice_rows)]
-        for d in range(1, n_z):
-            d1_copy(lax.rem(z + d, n_z), z).start()
+        for h in range(halves):
+            diag_half(dpart, h)
+            drec[z, h] = dpart[h, pl.ds(pl.multiple_of(z * slice_rows, slice_rows), slice_rows)]
+            for d in range(1, n_z):
+                d1_copy(lax.rem(z + d, n_z), z, h).start()
 
     @pl.when(late_owner)
     def _():
@@ -435,49 +473,40 @@
     def _():
         for h in range(halves):
             froot_t[h * H:(h + 1) * H, :] = jnp.transpose(fbuf[late, h])
-        for h in range(halves):
-            for r in range(2):
-                pall[pl.ds(starts[r], rows), h * H:(h + 1) * H] = late_total(r, h).astype(jnp.bfloat16)
-        late_dpart[...] = jnp.dot(
-            froot_t[...], pall[...], preferred_element_type=jnp.float32
-        ).astype(jnp.bfloat16)
-        for to in range(n_z):
-            late_d1(to).start()
-
-    value = jnp.zeros((slice_rows, B), jnp.float32)
-    for q in range(n_z):
-        @pl.when((q != z) | late_owner)
-        def _():
-            d1_copy(q, q).wait_recv()
-        value = value + drec[q].astype(jnp.float32)
-    dall[c] = value.astype(jnp.bfloat16)
-
-    def d2_copy(to, own):
-        return remote(dall.at[own], dall.at[own], d2_s.at[to], d2_r.at[own], p, to)
-
-    for d in range(1, n_z * n_x):
-        d2_copy(lax.rem(c + d, n_z * n_x), c).start()
+
+    for h in range(1, halves):
+        late_half(h)
+
+    def d2_copy(to, own, h):
+        return remote(dall.at[own, h], dall.at[own, h], d2_s.at[to, h], d2_r.at[own, h], p, to)
+
+    for h in range(halves):
+        value = jnp.zeros((slice_rows, H), jnp.float32)
+        for q in range(n_z):
+            @pl.when((q != z) | late_owner)
+            def _():
+                d1_copy(q, q, h).wait_recv()
+            value = value + drec[q, h].astype(jnp.float32)
+        dall[c, h] = value.astype(jnp.bfloat16)
+        for d in range(1, n_z * n_x):
+            d2_copy(lax.rem(c + d, n_z * n_x), c, h).start()
 
     for h in range(halves):
         x_copy(h).wait_recv()
         write(pnb[h].astype(jnp.float32), 1, h)
 
-    def corner(w, r):
-        wide = wid_ref[2 * p + w]
-        shape = (slice_rows, B)
-        line = lax.broadcasted_iota(jnp.int32, shape, 0) + r * slice_rows
-        col = lax.broadcasted_iota(jnp.int32, shape, 1)
-        own = dinv_ref[r * slice_rows:(r + 1) * slice_rows, w * B:(w + 1) * B]
-        return jnp.where((line < wide) & (col < wide), own, 0.0)
-
-    for d in range(1, n_z * n_x):
-        q = lax.rem(c + d, n_z * n_x)
-        d2_copy(q, q).wait_recv()
+    for h in range(halves):
+        for d in range(1, n_z * n_x):
+            q = lax.rem(c + d, n_z * n_x)
+            d2_copy(q, q, h).wait_recv()
     for r in range(n_z):
         for w in range(n_x):
-            diag_ref[r * slice_rows:(r + 1) * slice_rows, w * B:(w + 1) * B] = (
-                corner(w, r) + dall[r * n_x + w].astype(jnp.float32)
-            )
+            for h in range(halves):
+                diag_ref[r * slice_rows:(r + 1) * slice_rows, w * B + h * H:w * B + (h + 1) * H] += (
+                    dall[r * n_x + w, h].astype(jnp.float32)
+                )
+    diag_copy = pltpu.make_async_copy(diag_ref, diag_hbm, out_s.at[2, 0])
+    diag_copy.start()
 
     a_copy.wait_send()
     for h in range(halves):
@@ -519,17 +548,22 @@
                 pair_copy(s % 2, h).wait_send()
                 cross_copy(s % 2, core, h).wait_send()
 
-    @pl.when(jnp.logical_not(late_owner))
-    def _():
-        for d in range(1, n_z):
-            d1_copy(lax.rem(z + d, n_z), z).wait_send()
-
-    @pl.when(late_root)
-    def _():
-        for to in range(n_z):
-            late_d1(to).wait_send()
-    for d in range(1, n_z * n_x):
-        d2_copy(lax.rem(c + d, n_z * n_x), c).wait_send()
+    for h in range(halves):
+        @pl.when(jnp.logical_not(late_owner))
+        def _():
+            for d in range(1, n_z):
+                d1_copy(lax.rem(z + d, n_z), z, h).wait_send()
+
+        @pl.when(late_root)
+        def _():
+            for to in range(n_z):
+                late_d1(to, h).wait_send()
+
+        for d in range(1, n_z * n_x):
+            d2_copy(lax.rem(c + d, n_z * n_x), c, h).wait_send()
+        for w in range(2):
+            sel_copy(w, h).wait()
+    diag_copy.wait()
 
 
 def fused(n_prow, n_pcol, ainv, lpanel, dinv, rowblocks, counts, widths):
@@ -537,7 +571,6 @@
     rows, depth = ainv.shape
     bf, f32, H = jnp.bfloat16, jnp.float32, 128
     halves = B // H
-    vmem = pl.BlockSpec(memory_space=pltpu.VMEM)
     hbm = pl.BlockSpec(memory_space=pltpu.HBM)
     dma = pltpu.SemaphoreType.DMA
     piece = (2, halves, rows, H)
@@ -548,8 +581,10 @@
             jax.ShapeDtypeStruct(dinv.shape, f32),
         ),
         in_specs=[hbm] * 6,
-        out_specs=(vmem, vmem),
+        out_specs=(hbm, hbm),
         scratch_shapes=[
+            pltpu.VMEM((rows, dinv.shape[1]), bf),
+            pltpu.VMEM(dinv.shape, f32),
             pltpu.VMEM((2, rows, depth), bf),
             pltpu.VMEM(lpanel.shape, bf),
             pltpu.VMEM(dinv.shape, f32),
@@ -567,15 +602,15 @@
             pltpu.VMEM((depth, B), bf),
             pltpu.VMEM((halves, rows, H), bf),
             pltpu.VMEM((halves, rows, H), bf),
-            pltpu.VMEM((B, B), bf),
-            pltpu.VMEM((n_z, B // n_z, B), bf),
-            pltpu.VMEM((n_z * n_x, B // n_z, B), bf),
+            pltpu.VMEM((halves, B, H), bf),
+            pltpu.VMEM((n_z, halves, B // n_z, H), bf),
+            pltpu.VMEM((n_z * n_x, halves, B // n_z, H), bf),
             pltpu.VMEM((halves, rows, H), f32),
             pltpu.VMEM((halves, rows, H), bf),
             pltpu.VMEM((halves, rows, H), bf),
             pltpu.VMEM((halves, rows, H), bf),
             pltpu.VMEM((2, 2, halves, rows, H), bf),
-            pltpu.VMEM((B, B), bf),
+            pltpu.VMEM((halves, B, H), bf),
             dma((6,)),
             dma((2,)),
             dma((2, n_z, halves)),
@@ -587,15 +622,16 @@
         + [
             dma((halves,)),
             dma((halves,)),
-            dma((n_z,)),
-            dma((n_z,)),
-            dma((n_z * n_x,)),
-            dma((n_z * n_x,)),
+            dma((n_z, halves)),
+            dma((n_z, halves)),
+            dma((n_z * n_x, halves)),
+            dma((n_z * n_x, halves)),
             dma((halves,)),
             dma((halves,)),
             dma((2, halves)),
             dma((2, 2, halves)),
-            dma((n_z,)),
+            dma((n_z, halves)),
+            dma((3, halves)),
         ],
         compiler_params=pltpu.CompilerParams(
             collective_id=0, has_side_effects=True, vmem_limit_bytes=60 * 1024 * 1024

time: 61.7 us -> 60.8 us (0.985)
  Pallas kernels: 60.9 us -> 60 us
    pallas_call x1, Pallas kernels: 58.9 us -> 58 us  [fused(): pl.pallas_call(functools.partial(level_kernel, n_z, n_x), out_shape=(jax....]
where the time goes in v5:
time: 60.8 us; the launch traced here: 60.7 us
  Pallas kernels  60 us (99%)
  between operations  0.64 us (1%)
    pallas_call x1, Pallas kernels, fused(): pl.pallas_call(functools.partial(level_kernel, n_z, n_x), out_shape=(jax....  58 us
    pallas_call x1, Pallas kernels, fused(): pl.pallas_call(handoff_kernel, out_shape=tuple((jax.ShapeDtypeStruct(r.sh...  1.98 us

profile of v5, /device:TPU:0, one launch (start us, length us, event | category | flops | bytes accessed | tf_op | source)
XLA Modules:
  0.0 60.7 jit_solution(387931097829871872)
XLA Ops:
  0.6 58.0 %shard_map.77 = (bf16[512,512]{1,0:T(8,128)(2,1)}, f32[256,512]{1,0:T(8,128)}) custom-call(bf16[512,1024]{1,0:T(8,128)(2,1)} %a_hbm.1, bf16[1024,256]{1,0:T(8,128)(2,1)} %lp_hbm.1, f32[256,512]{1,0:T(8,128)} %dinv_hbm.1, s32[8,10]{1,0:T(8,128)} %rb_hbm.1, s32[8]{0:T(128)} %cnt_hbm.1, s32[8]{0:T(128)} %wid_hbm.1), custom_call_target="tpu_custom_call" | custom-call | flops 2147483648 | bytes 4194304 | tf_op jit(solution)/shard_map/pallas_call | solution.py:577
  58.7 2.0 %shard_map.78 = (bf16[512,512]{1,0:T(8,128)(2,1)}, f32[256,512]{1,0:T(8,128)}) custom-call(bf16[512,512]{1,0:T(8,128)(2,1)} %get-tuple-element.4.sel_in, f32[256,512]{1,0:T(8,128)} %get-tuple-element.5.diag_in), custom_call_target="tpu_custom_call" | custom-call | tf_op jit(solution)/shard_map/pallas_call | solution.py:644

commit v6 on v5

--- a/solution.py
+++ b/solution.py
@@ -165,7 +165,7 @@
     for d in range(n_z):
         pl.semaphore_signal(barrier, inc=1, device_id=(p, d * n_x + xo), device_id_type=MESH)
 
-    a_copy = remote(a_hbm, a_buf.at[1], a_sem.at[0], a_sem.at[1], p, z * n_x + xo)
+    a_copy = remote(a_buf.at[0], a_buf.at[1], a_sem.at[0], a_sem.at[1], p, z * n_x + xo)
 
     def f_copy(s, h, way):
         return remote(
@@ -243,6 +243,7 @@
             value = lp_ref[b * B:(b + 1) * B, h * H:(h + 1) * H].astype(jnp.float32)
             fbuf[z, h, b * B:(b + 1) * B, :] = jnp.where(cols < limits[b], value, 0.0).astype(jnp.bfloat16)
         if h == 0:
+            fetches[4].wait()
             pl.semaphore_wait(barrier, n_z * n_z - 1 + n_z)
             a_copy.start()
 
@@ -253,8 +254,7 @@
         @pl.when(z > 0)
         def _():
             f_copy(z, h, 1).start()
-    for fetch in fetches[4:]:
-        fetch.wait()
+    fetches[5].wait()
 
     def both(j, act):
         t = lax.div(j, halves)
@@ -400,7 +400,6 @@
         both(j, third_act)
         return carry
 
-    lax.fori_loop(early, early + halves, third, 0)
 
     def total(r, h):
         part_copy(r, h).wait_recv()
@@ -435,12 +434,7 @@
             for to in range(n_z):
                 late_d1(to, h).start()
 
-    @pl.when(late_root)
-    def _():
-        for h in range(halves):
-            froot_t[h * H:(h + 1) * H, :] = jnp.transpose(fbuf[late, h])
-
-    late_half(0)
+    lax.fori_loop(early, early + 1, third, 0)
 
     @pl.when(jnp.logical_not(late_owner))
     def _():
@@ -462,17 +456,21 @@
             for d in range(1, n_z):
                 d1_copy(lax.rem(z + d, n_z), z, h).start()
 
+    lax.fori_loop(early + 1, early + halves, third, 0)
+
+    @pl.when(late_root)
+    def _():
+        for h in range(halves):
+            froot_t[h * H:(h + 1) * H, :] = jnp.transpose(fbuf[late, h])
+
+    late_half(0)
+
     @pl.when(late_owner)
     def _():
         for h in range(halves):
             pbf[h] = late_total(1, h).astype(jnp.bfloat16)
             x_copy(h).start()
             write(late_total(0, h), 0, h)
-
-    @pl.when(late_root)
-    def _():
-        for h in range(halves):
-            froot_t[h * H:(h + 1) * H, :] = jnp.transpose(fbuf[late, h])
 
     for h in range(1, halves):
         late_half(h)

time: 60.8 us -> 61.5 us (1.012); the launches traced: 60.7 us -> 60.5 us
  no operation moved by 1% of the time
where the time goes in v6:
time: 61.5 us; the launch traced here: 60.5 us
  Pallas kernels  59.8 us (97%)
  between operations  0.64 us (1%)
    pallas_call x1, Pallas kernels, fused(): pl.pallas_call(functools.partial(level_kernel, n_z, n_x), out_shape=(jax....  57.9 us
    pallas_call x1, Pallas kernels, fused(): pl.pallas_call(handoff_kernel, out_shape=tuple((jax.ShapeDtypeStruct(r.sh...  1.98 us

profile of v6, /device:TPU:0, one launch (start us, length us, event | category | flops | bytes accessed | tf_op | source)
XLA Modules:
  0.0 60.5 jit_solution(12767854776305390143)
XLA Ops:
  0.6 57.9 %shard_map.77 = (bf16[512,512]{1,0:T(8,128)(2,1)}, f32[256,512]{1,0:T(8,128)}) custom-call(bf16[512,1024]{1,0:T(8,128)(2,1)} %a_hbm.1, bf16[1024,256]{1,0:T(8,128)(2,1)} %lp_hbm.1, f32[256,512]{1,0:T(8,128)} %dinv_hbm.1, s32[8,10]{1,0:T(8,128)} %rb_hbm.1, s32[8]{0:T(128)} %cnt_hbm.1, s32[8]{0:T(128)} %wid_hbm.1), custom_call_target="tpu_custom_call" | custom-call | flops 2147483648 | bytes 4194304 | tf_op jit(solution)/shard_map/pallas_call | solution.py:575
  58.5 2.0 %shard_map.78 = (bf16[512,512]{1,0:T(8,128)(2,1)}, f32[256,512]{1,0:T(8,128)}) custom-call(bf16[512,512]{1,0:T(8,128)(2,1)} %get-tuple-element.4.sel_in, f32[256,512]{1,0:T(8,128)} %get-tuple-element.5.diag_in), custom_call_target="tpu_custom_call" | custom-call | tf_op jit(solution)/shard_map/pallas_call | solution.py:642

commit v7 on v5

--- a/solution.py
+++ b/solution.py
@@ -165,7 +165,7 @@
     for d in range(n_z):
         pl.semaphore_signal(barrier, inc=1, device_id=(p, d * n_x + xo), device_id_type=MESH)
 
-    a_copy = remote(a_hbm, a_buf.at[1], a_sem.at[0], a_sem.at[1], p, z * n_x + xo)
+    a_copy = remote(a_buf.at[0], a_buf.at[1], a_sem.at[0], a_sem.at[1], p, z * n_x + xo)
 
     def f_copy(s, h, way):
         return remote(
@@ -244,17 +244,19 @@
             fbuf[z, h, b * B:(b + 1) * B, :] = jnp.where(cols < limits[b], value, 0.0).astype(jnp.bfloat16)
         if h == 0:
             pl.semaphore_wait(barrier, n_z * n_z - 1 + n_z)
+
+        @pl.when(z < n_z - 1)
+        def _():
+            f_copy(z, h, 0).start()
+
+        @pl.when(z > 0)
+        def _():
+            f_copy(z, h, 1).start()
+
+        if h == 0:
+            fetches[4].wait()
             a_copy.start()
-
-        @pl.when(z < n_z - 1)
-        def _():
-            f_copy(z, h, 0).start()
-
-        @pl.when(z > 0)
-        def _():
-            f_copy(z, h, 1).start()
-    for fetch in fetches[4:]:
-        fetch.wait()
+    fetches[5].wait()
 
     def both(j, act):
         t = lax.div(j, halves)

time: 60.8 us -> 60.8 us (level)
  no operation moved by 1% of the time
where the time goes in v7:
time: 60.8 us; the launch traced here: 60.7 us
  Pallas kernels  60 us (99%)
  between operations  0.64 us (1%)
    pallas_call x1, Pallas kernels, fused(): pl.pallas_call(functools.partial(level_kernel, n_z, n_x), out_shape=(jax....  58 us
    pallas_call x1, Pallas kernels, fused(): pl.pallas_call(handoff_kernel, out_shape=tuple((jax.ShapeDtypeStruct(r.sh...  1.98 us

profile of v7, /device:TPU:0, one launch (start us, length us, event | category | flops | bytes accessed | tf_op | source)
XLA Modules:
  0.0 60.7 jit_solution(16676632916148567851)
XLA Ops:
  0.6 58.0 %shard_map.77 = (bf16[512,512]{1,0:T(8,128)(2,1)}, f32[256,512]{1,0:T(8,128)}) custom-call(bf16[512,1024]{1,0:T(8,128)(2,1)} %a_hbm.1, bf16[1024,256]{1,0:T(8,128)(2,1)} %lp_hbm.1, f32[256,512]{1,0:T(8,128)} %dinv_hbm.1, s32[8,10]{1,0:T(8,128)} %rb_hbm.1, s32[8]{0:T(128)} %cnt_hbm.1, s32[8]{0:T(128)} %wid_hbm.1), custom_call_target="tpu_custom_call" | custom-call | flops 2147483648 | bytes 4194304 | tf_op jit(solution)/shard_map/pallas_call | solution.py:579
  58.7 2.0 %shard_map.78 = (bf16[512,512]{1,0:T(8,128)(2,1)}, f32[256,512]{1,0:T(8,128)}) custom-call(bf16[512,512]{1,0:T(8,128)(2,1)} %get-tuple-element.4.sel_in, f32[256,512]{1,0:T(8,128)} %get-tuple-element.5.diag_in), custom_call_target="tpu_custom_call" | custom-call | tf_op jit(solution)/shard_map/pallas_call | solution.py:646

commit v8 on v5

--- a/solution.py
+++ b/solution.py
@@ -233,6 +233,15 @@
             def _():
                 froot[h] = fbuf[s, h]
 
+    def own_send(h):
+        @pl.when(z < n_z - 1)
+        def _():
+            f_copy(z, h, 0).start()
+
+        @pl.when(z > 0)
+        def _():
+            f_copy(z, h, 1).start()
+
     for fetch in fetches[:4]:
         fetch.wait()
     width = wid_ref[c]
@@ -244,15 +253,8 @@
             fbuf[z, h, b * B:(b + 1) * B, :] = jnp.where(cols < limits[b], value, 0.0).astype(jnp.bfloat16)
         if h == 0:
             pl.semaphore_wait(barrier, n_z * n_z - 1 + n_z)
+            own_send(0)
             a_copy.start()
-
-        @pl.when(z < n_z - 1)
-        def _():
-            f_copy(z, h, 0).start()
-
-        @pl.when(z > 0)
-        def _():
-            f_copy(z, h, 1).start()
     for fetch in fetches[4:]:
         fetch.wait()
 
@@ -295,6 +297,10 @@
         @pl.when(j < early)
         def _():
             both(j, lambda t, h, way, s: partial(s, 0, h))
+
+        @pl.when(j < halves - 1)
+        def _():
+            own_send(j + 1)
 
         return carry
 

time: 60.8 us -> 60.8 us (level)
  no operation moved by 1% of the time
where the time goes in v8:
time: 60.8 us; the launch traced here: 60.7 us
  Pallas kernels  60 us (99%)
  between operations  0.64 us (1%)
    pallas_call x1, Pallas kernels, fused(): pl.pallas_call(functools.partial(level_kernel, n_z, n_x), out_shape=(jax....  58 us
    pallas_call x1, Pallas kernels, fused(): pl.pallas_call(handoff_kernel, out_shape=tuple((jax.ShapeDtypeStruct(r.sh...  1.98 us

profile of v8, /device:TPU:0, one launch (start us, length us, event | category | flops | bytes accessed | tf_op | source)
XLA Modules:
  0.0 60.7 jit_solution(11629981508209572424)
XLA Ops:
  0.6 58.0 %shard_map.77 = (bf16[512,512]{1,0:T(8,128)(2,1)}, f32[256,512]{1,0:T(8,128)}) custom-call(bf16[512,1024]{1,0:T(8,128)(2,1)} %a_hbm.1, bf16[1024,256]{1,0:T(8,128)(2,1)} %lp_hbm.1, f32[256,512]{1,0:T(8,128)} %dinv_hbm.1, s32[8,10]{1,0:T(8,128)} %rb_hbm.1, s32[8]{0:T(128)} %cnt_hbm.1, s32[8]{0:T(128)} %wid_hbm.1), custom_call_target="tpu_custom_call" | custom-call | flops 2147483648 | bytes 4194304 | tf_op jit(solution)/shard_map/pallas_call | solution.py:583
  58.7 2.0 %shard_map.78 = (bf16[512,512]{1,0:T(8,128)(2,1)}, f32[256,512]{1,0:T(8,128)}) custom-call(bf16[512,512]{1,0:T(8,128)(2,1)} %get-tuple-element.4.sel_in, f32[256,512]{1,0:T(8,128)} %get-tuple-element.5.diag_in), custom_call_target="tpu_custom_call" | custom-call | tf_op jit(solution)/shard_map/pallas_call | solution.py:650
